TPU v7x, 512 devices: a whole 4x8x8 slice. The times are simulated.
512 devices in a mesh: gx: 32 (over x, z_lo, core), gy: 16 (over z_hi, y).
Axes of the slice: x: 4, y: 8, z: 8 (z_hi: 2, z_lo: 4; z = z_hi * 4 + z_lo), core: 2. Of those that a mesh axis runs over, the one named last changes fastest.
Arguments:
- features: bfloat16 [32, 512, 4096], P(None, 'gx', 'gy'), may hold values from -6 to 6
- brick_mask: int32 [32, 16, 1], P('gx', 'gy'), may hold values 0 or 1
- kernel_fine: bfloat16 [27, 1024], replicated, may hold values from -0.21875 to 0.21875
- kernel_down: bfloat16 [8, 2048], replicated, may hold values from -0.375 to 0.375
- kernel_coarse: bfloat16 [27, 4096], replicated, may hold values from -0.15625 to 0.15625
- cotangent: bfloat16 [64, 256, 1024], P(None, 'gx', 'gy'), may hold values from -24 to 24
Outputs:
- grad_features: bfloat16 [32, 512, 4096], P(None, 'gx', 'gy')
All inputs are finite; a program needn't handle non-finite values. No bound on the sum of `brick_mask` on one device may be relied on, other than what follows from the above.
Results may differ from a plain program's by a relative error of at most 0.014.
Values may be sent and summed in bfloat16 or wider, within the bound.
No kernel may reach another device: no remote copies, remote signals or barrier semaphores. Data moves between devices by JAX's collectives and lax.ppermute only.
A program may use at most 64 MiB of HBM per device.

v0:
```python
import jax
import jax.numpy as jnp
from jax import lax
from jax.sharding import PartitionSpec as P

layout = ("NCDHW", "OIDHW", "NCDHW")


def extended(cells, sides, width):
    for axis, dim in sides:
        count = lax.axis_size(axis)
        ends = count - 1
        head = lax.slice_in_dim(cells, 0, width, axis=dim)
        tail = lax.slice_in_dim(cells, cells.shape[dim] - width, cells.shape[dim], axis=dim)
        cells = jnp.concatenate(
            [
                lax.ppermute(tail, axis, [(i, (i + 1) % count) for i in range(ends)]),
                cells,
                lax.ppermute(head, axis, [((i + 1) % count, i) for i in range(ends)]),
            ],
            axis=dim,
        )
    return cells


def unpack_kernel(kernel, side, size_out, size_in):
    return kernel.reshape(side, side, side, size_out, size_in).transpose(3, 4, 0, 1, 2)


def conv_local(padded, kernel):
    return lax.conv_general_dilated(
        padded[None],
        kernel,
        (1, 1, 1),
        "VALID",
        dimension_numbers=layout,
        preferred_element_type=jnp.float32,
    )[0]


def depth_pad(volume):
    return jnp.pad(volume, ((0, 0), (0, 0), (0, 0), (1, 1)))


def flipped(kernel):
    return jnp.flip(kernel, (2, 3, 4)).transpose(1, 0, 2, 3, 4)


def reduce_down(field, kernel):
    return lax.conv_general_dilated(
        field[None],
        kernel,
        (2, 2, 2),
        "VALID",
        dimension_numbers=layout,
        preferred_element_type=jnp.float32,
    )[0]


def spread_up(gradient, kernel):
    product = jnp.einsum(
        "ocabe,oxyz->cxaybze", kernel, gradient, preferred_element_type=jnp.float32
    )
    shape = product.shape
    return product.reshape(shape[0], shape[1] * 2, shape[3] * 2, shape[5] * 2)


def derivative(value):
    logistic = jax.nn.sigmoid(value)
    return logistic * (1.0 + value * (1.0 - logistic))


def brick_cells(flags, repeat_by):
    grown = jnp.repeat(jnp.repeat(jnp.repeat(flags, repeat_by, 0), repeat_by, 1), repeat_by, 2)
    return grown.astype(jnp.float32)


def on_device(features, brick_mask, kernel_fine, kernel_down, kernel_coarse, cotangent):
    chan_fine = features.shape[0]
    chan_coarse = cotangent.shape[0]
    brick = features.shape[1] // brick_mask.shape[0]
    depth = brick * brick_mask.shape[2]
    rows_x = features.shape[1]
    rows_y = features.shape[2] // depth
    features = features.reshape(chan_fine, rows_x, rows_y, depth)
    cotangent = cotangent.reshape(chan_coarse, rows_x // 2, rows_y // 2, depth // 2)
    kernel_fine = unpack_kernel(kernel_fine, 3, chan_fine, chan_fine)
    kernel_down = unpack_kernel(kernel_down, 2, chan_coarse, chan_fine)
    kernel_coarse = unpack_kernel(kernel_coarse, 3, chan_coarse, chan_coarse)
    fine_flags = brick_cells(brick_mask, brick)
    coarse_flags = brick_cells(brick_mask, brick // 2)
    rim_field = extended(features, (("gx", 1), ("gy", 2)), 1)
    pre_fine = conv_local(depth_pad(rim_field), kernel_fine)
    hidden = (fine_flags * jax.nn.silu(pre_fine)).astype(jnp.bfloat16)
    down_field = reduce_down(hidden, kernel_down).astype(jnp.bfloat16)
    rim_coarse = extended(down_field, (("gx", 1), ("gy", 2)), 1)
    pre_coarse = conv_local(depth_pad(rim_coarse), kernel_coarse)
    grad_coarse = (cotangent.astype(jnp.float32) * coarse_flags * derivative(pre_coarse)).astype(
        jnp.bfloat16
    )
    grad_rim = extended(grad_coarse, (("gx", 1), ("gy", 2)), 1)
    grad_down = conv_local(depth_pad(grad_rim), flipped(kernel_coarse)).astype(jnp.bfloat16)
    grad_fine = (spread_up(grad_down, kernel_down) * fine_flags * derivative(pre_fine)).astype(
        jnp.bfloat16
    )
    grad_rim_fine = extended(grad_fine, (("gx", 1), ("gy", 2)), 1)
    result = conv_local(depth_pad(grad_rim_fine), flipped(kernel_fine)).astype(jnp.bfloat16)
    return result.reshape(chan_fine, rows_x, rows_y * depth)


def solution(mesh):
    placed = (P(None, "gx", "gy"), P("gx", "gy", None), P(), P(), P(), P(None, "gx", "gy"))
    return jax.shard_map(
        on_device, mesh=mesh, in_specs=placed, out_specs=P(None, "gx", "gy"), check_vma=False
    )
```

profile of v0, /device:TPU:62, one launch (start us, length us, event | category | flops | bytes accessed | tf_op | source)
XLA Modules:
  0.0 154.1 jit_solution(11151285110915045395)
XLA Ops:
  0.0 1.5 copy.12
  1.5 1.9 %collective-permute-start = (bf16[32,1,16,16]{0,3,2,1:T(8,128)(2,1)S(1)}, bf16[32,1,16,16]{0,3,2,1:T(8,128)(2,1)S(1)}, u32[]{:S(2)}, u32[]{:S(2)}) collective-permute-start(bf16[32,1,16,16]{0,3,2,1:T(8,128)(2,1)S(1)} %get-tuple-element.11), channel_id=1, source_target_pairs={{0,16},{16,32},{32,48},{48,64},{64,80},{80,96},{96,112},{112,128},... | collective-permute-start | bytes 49160 | tf_op jit(solution)/shard_map/ppermute | solution.py:17
  3.5 7.6 %collective-permute-start.1 = (bf16[32,1,16,16]{0,3,2,1:T(8,128)(2,1)S(1)}, bf16[32,1,16,16]{0,3,2,1:T(8,128)(2,1)S(1)}, u32[]{:S(2)}, u32[]{:S(2)}) collective-permute-start(bf16[32,1,16,16]{0,3,2,1:T(8,128)(2,1)S(1)} %get-tuple-element.12), channel_id=1, source_target_pairs={{16,0},{32,16},{48,32},{64,48},{80,64},{96,80},{112,96},{128,112},... | collective-permute-start | bytes 49160 | tf_op jit(solution)/shard_map/ppermute | solution.py:19
  11.1 1.9 %collective-permute-done.1 = bf16[32,1,16,16]{0,3,2,1:T(8,128)(2,1)S(1)} collective-permute-done((bf16[32,1,16,16]{0,3,2,1:T(8,128)(2,1)S(1)}, bf16[32,1,16,16]{0,3,2,1:T(8,128)(2,1)S(1)}, u32[]{:S(2)}, u32[]{:S(2)}) %collective-permute-start.1) | collective-permute-done | bytes 16416 | tf_op jit(solution)/shard_map/ppermute | solution.py:19
  13.0 8.9 %collective-permute-start.2 = (bf16[32,18,1,16]{0,3,2,1:T(8,128)(2,1)S(1)}, bf16[32,18,1,16]{0,3,2,1:T(8,128)(2,1)S(1)}, u32[]{:S(2)}, u32[]{:S(2)}) collective-permute-start(bf16[32,18,1,16]{0,3,2,1:T(8,128)(2,1)S(1)} %get-tuple-element.7), channel_id=1, source_target_pairs={{0,1},{1,2},{2,3},{3,4},{4,5},{5,6},{6,7},{7,8},{8,9},{9,10},{10,1... | collective-permute-start | bytes 55304 | tf_op jit(solution)/shard_map/ppermute | solution.py:17
  21.9 1.9 %collective-permute-start.3 = (bf16[32,18,1,16]{0,3,2,1:T(8,128)(2,1)S(1)}, bf16[32,18,1,16]{0,3,2,1:T(8,128)(2,1)S(1)}, u32[]{:S(2)}, u32[]{:S(2)}) collective-permute-start(bf16[32,18,1,16]{0,3,2,1:T(8,128)(2,1)S(1)} %get-tuple-element.8), channel_id=1, source_target_pairs={{1,0},{2,1},{3,2},{4,3},{5,4},{6,5},{7,6},{8,7},{9,8},{10,9},{11,1... | collective-permute-start | bytes 55304 | tf_op jit(solution)/shard_map/ppermute | solution.py:19
  24.4 0.9 reshape.34
  25.5 8.6 %collective-permute-done.3 = bf16[32,18,1,16]{0,3,2,1:T(8,128)(2,1)S(1)} collective-permute-done((bf16[32,18,1,16]{0,3,2,1:T(8,128)(2,1)S(1)}, bf16[32,18,1,16]{0,3,2,1:T(8,128)(2,1)S(1)}, u32[]{:S(2)}, u32[]{:S(2)}) %collective-permute-start.3) | collective-permute-done | bytes 18464 | tf_op jit(solution)/shard_map/ppermute | solution.py:19
  34.1 1.7 %fusion.19 = bf16[32,18,18,1,18]{0,4,2,1,3:T(8,128)(2,1)S(1)} fusion(bf16[32,18,1,16]{0,3,2,1:T(8,128)(2,1)S(1)} %collective-permute-done.3, bf16[32,18,1,16]{0,3,2,1:T(8,128)(2,1)S(1)} %collective-permute-done.2, bf16[32,1,16,16]{0,3,2,1:T(8,128)(2,1)S(1)} %collective-permute-done.1, bf16[32,16,16,16]{0,3,2,1:T(8,128)(2,1)S(1)} %bitcast.81, ...), kind=kLoop, calls=%fused_computation.31 | loop fusion | flops 3359232 | bytes 705024 | tf_op jit(solution)/shard_map/broadcast_in_dim | solution.py:32
  35.9 1.7 %pad.18 = bf16[32,18,18,1,24]{0,4,2,1,3:T(8,128)(2,1)} pad(bf16[32,18,18,1,18]{0,4,2,1,3:T(8,128)(2,1)S(1)} %fusion.19, bf16[]{:T(256)} %constant.3.clone.1), padding=0_0x0_0x0_0x0_0x0_6 | pad | bytes 870914 | tf_op jit(solution)/shard_map/broadcast_in_dim | solution.py:32
  37.6 5.1 %reshape.39 = bf16[32,18,18,1,8,3]{0,5,4,2,1,3:T(4,128)(2,1)S(1)} reshape(bf16[32,18,18,1,24]{0,4,2,1,3:T(8,128)(2,1)} %pad.18) | data formatting | bytes 995328 | tf_op jit(solution)/shard_map/conv_general_dilated | solution.py:31
  43.4 0.6 copy-done.3
  44.0 5.0 %fusion.36 = (bf16[16,16,8,3,32]{4,2,3,1,0:T(8,128)(2,1)S(1)}, f32[16,16,8,3,32]{4,2,3,1,0:T(8,128)S(1)}) fusion(f32[]{:T(128)} %bitcast, pred[8,3]{0,1:T(4,128)(4,1)S(1)} %copy-done.9, bf16[3,3,3,32,32]{4,3,2,1,0:T(8,128)(2,1)S(1)} %copy-done.3, bf16[32,18,18,1,7,2]{0,4,5,2,1,3:T(8,128)(2,1)S(1)} %slice.73, bf16[32,18,18,1,8,3]{0,4,5,2,1,3:T(8,128)(2,1)S(1)} %copy.14), kind=kOutput, calls=%fused_computation.44 | convolution fusion | flops 343799808 | bytes 2022940 | tf_op jit(solution)/shard_map/conv_general_dilated | solution.py:31
  50.3 0.6 fusion.40
  50.9 1.9 %collective-permute-start.4 = (bf16[64,1,8,8]{0,3,2,1:T(8,128)(2,1)S(1)}, bf16[64,1,8,8]{0,3,2,1:T(8,128)(2,1)S(1)}, u32[]{:S(2)}, u32[]{:S(2)}) collective-permute-start(bf16[64,1,8,8]{0,3,2,1:T(8,128)(2,1)S(1)} %get-tuple-element.19), channel_id=1, source_target_pairs={{0,16},{16,32},{32,48},{48,64},{64,80},{80,96},{96,112},{112,128},... | collective-permute-start | bytes 24584 | tf_op jit(solution)/shard_map/ppermute | solution.py:17
  52.8 6.3 %collective-permute-start.5 = (bf16[64,1,8,8]{0,3,2,1:T(8,128)(2,1)S(1)}, bf16[64,1,8,8]{0,3,2,1:T(8,128)(2,1)S(1)}, u32[]{:S(2)}, u32[]{:S(2)}) collective-permute-start(bf16[64,1,8,8]{0,3,2,1:T(8,128)(2,1)S(1)} %get-tuple-element.20), channel_id=1, source_target_pairs={{16,0},{32,16},{48,32},{64,48},{80,64},{96,80},{112,96},{128,112},... | collective-permute-start | bytes 24584 | tf_op jit(solution)/shard_map/ppermute | solution.py:19
  59.2 1.4 collective-permute-done.5
  60.6 0.6 pad_maximum_fusion.11
  61.2 1.9 %collective-permute-start.6 = (bf16[64,10,1,8]{0,3,2,1:T(8,128)(2,1)}, bf16[64,10,1,8]{0,3,2,1:T(8,128)(2,1)}, u32[]{:S(2)}, u32[]{:S(2)}) collective-permute-start(bf16[64,10,1,8]{0,3,2,1:T(8,128)(2,1)} %get-tuple-element.15), channel_id=1, source_target_pairs={{0,1},{1,2},{2,3},{3,4},{4,5},{5,6},{6,7},{7,8},{8,9},{9,10},{10,1... | collective-permute-start | bytes 30728 | tf_op jit(solution)/shard_map/ppermute | solution.py:17
  63.1 4.1 %collective-permute-start.7 = (bf16[64,10,1,8]{0,3,2,1:T(8,128)(2,1)}, bf16[64,10,1,8]{0,3,2,1:T(8,128)(2,1)}, u32[]{:S(2)}, u32[]{:S(2)}) collective-permute-start(bf16[64,10,1,8]{0,3,2,1:T(8,128)(2,1)} %get-tuple-element.16), channel_id=1, source_target_pairs={{1,0},{2,1},{3,2},{4,3},{5,4},{6,5},{7,6},{8,7},{9,8},{10,9},{11,1... | collective-permute-start | bytes 30728 | tf_op jit(solution)/shard_map/ppermute | solution.py:19
  67.3 0.7 convert_multiply_fusion
  68.0 2.2 %reshape.36 = bf16[3,3,3,64,64]{4,3,2,1,0:T(8,128)(2,1)} reshape(bf16[27,4096]{1,0:T(8,128)(2,1)} %param.10) | data formatting | bytes 442368 | tf_op jit(solution)/shard_map/reshape | solution.py:27
  70.2 1.1 copy.11
  71.3 3.9 %collective-permute-done.7 = bf16[64,10,1,8]{0,3,2,1:T(8,128)(2,1)} collective-permute-done((bf16[64,10,1,8]{0,3,2,1:T(8,128)(2,1)}, bf16[64,10,1,8]{0,3,2,1:T(8,128)(2,1)}, u32[]{:S(2)}, u32[]{:S(2)}) %collective-permute-start.7) | collective-permute-done | bytes 10272 | tf_op jit(solution)/shard_map/ppermute | solution.py:19
  75.2 1.0 fusion.59
  76.1 6.5 %fusion.46 = f32[1,64,8,8,8]{1,0,4,3,2:T(1,128)S(1)} fusion(bf16[3,3,3,64,64]{4,3,2,1,0:T(8,128)(2,1)} %reshape.36, bf16[1,64,10,10,10]{1,4,3,2,0:T(8,128)(2,1)S(1)} %fusion.59), kind=kOutput, calls=%fused_computation.54 | convolution fusion | flops 113246208 | bytes 480256 | tf_op jit(solution)/shard_map/conv_general_dilated | solution.py:31
  82.8 1.9 %collective-permute-start.8 = (bf16[64,1,8,8]{0,3,2,1:T(8,128)(2,1)S(1)}, bf16[64,1,8,8]{0,3,2,1:T(8,128)(2,1)S(1)}, u32[]{:S(2)}, u32[]{:S(2)}) collective-permute-start(bf16[64,1,8,8]{0,3,2,1:T(8,128)(2,1)S(1)} %get-tuple-element.17), channel_id=1, source_target_pairs={{0,16},{16,32},{32,48},{48,64},{64,80},{80,96},{96,112},{112,128},... | collective-permute-start | bytes 24584 | tf_op jit(solution)/shard_map/ppermute | solution.py:17
  84.7 6.3 %collective-permute-start.9 = (bf16[64,1,8,8]{0,3,2,1:T(8,128)(2,1)S(1)}, bf16[64,1,8,8]{0,3,2,1:T(8,128)(2,1)S(1)}, u32[]{:S(2)}, u32[]{:S(2)}) collective-permute-start(bf16[64,1,8,8]{0,3,2,1:T(8,128)(2,1)S(1)} %get-tuple-element.18), channel_id=1, source_target_pairs={{16,0},{32,16},{48,32},{64,48},{80,64},{96,80},{112,96},{128,112},... | collective-permute-start | bytes 24584 | tf_op jit(solution)/shard_map/ppermute | solution.py:19
  91.1 1.4 collective-permute-done.9
  92.5 4.1 %collective-permute-start.10 = (bf16[64,10,1,8]{0,3,2,1:T(8,128)(2,1)S(1)}, bf16[64,10,1,8]{0,3,2,1:T(8,128)(2,1)S(1)}, u32[]{:S(2)}, u32[]{:S(2)}) collective-permute-start(bf16[64,10,1,8]{0,3,2,1:T(8,128)(2,1)S(1)} %get-tuple-element.13), channel_id=1, source_target_pairs={{0,1},{1,2},{2,3},{3,4},{4,5},{5,6},{6,7},{7,8},{8,9},{9,10},{10,1... | collective-permute-start | bytes 30728 | tf_op jit(solution)/shard_map/ppermute | solution.py:17
  96.6 1.9 %collective-permute-start.11 = (bf16[64,10,1,8]{0,3,2,1:T(8,128)(2,1)S(1)}, bf16[64,10,1,8]{0,3,2,1:T(8,128)(2,1)S(1)}, u32[]{:S(2)}, u32[]{:S(2)}) collective-permute-start(bf16[64,10,1,8]{0,3,2,1:T(8,128)(2,1)S(1)} %get-tuple-element.14), channel_id=1, source_target_pairs={{1,0},{2,1},{3,2},{4,3},{5,4},{6,5},{7,6},{8,7},{9,8},{10,9},{11,1... | collective-permute-start | bytes 30728 | tf_op jit(solution)/shard_map/ppermute | solution.py:19
  98.5 0.5 copy.22
  99.3 9.0 %collective-permute-done.11 = bf16[64,10,1,8]{0,3,2,1:T(8,128)(2,1)S(1)} collective-permute-done((bf16[64,10,1,8]{0,3,2,1:T(8,128)(2,1)S(1)}, bf16[64,10,1,8]{0,3,2,1:T(8,128)(2,1)S(1)}, u32[]{:S(2)}, u32[]{:S(2)}) %collective-permute-start.11) | collective-permute-done | bytes 10272 | tf_op jit(solution)/shard_map/ppermute | solution.py:19
  108.5 2.0 %convolution_convert_fusion = bf16[1,64,8,8,8]{1,0,4,3,2:T(2,128)(2,1)S(1)} fusion(bf16[3,3,3,64,64]{4,3,2,1,0:T(8,128)(2,1)S(1)} %copy-done.2, bf16[1,64,10,10,10]{1,4,3,2,0:T(8,128)(2,1)S(1)} %fusion.48), kind=kOutput, calls=%fused_computation.47 | convolution fusion | flops 113278976 | bytes 414720 | tf_op jit(solution)/shard_map/conv_general_dilated | solution.py:31
  110.9 1.2 copy.21
  112.1 1.1 multiply_convert_fusion.1
  113.3 1.9 %collective-permute-start.12 = (bf16[32,1,16,16]{0,3,2,1:T(8,128)(2,1)S(1)}, bf16[32,1,16,16]{0,3,2,1:T(8,128)(2,1)S(1)}, u32[]{:S(2)}, u32[]{:S(2)}) collective-permute-start(bf16[32,1,16,16]{0,3,2,1:T(8,128)(2,1)S(1)} %get-tuple-element.9), channel_id=1, source_target_pairs={{0,16},{16,32},{32,48},{48,64},{64,80},{80,96},{96,112},{112,128},... | collective-permute-start | bytes 49160 | tf_op jit(solution)/shard_map/ppermute | solution.py:17
  115.2 6.3 %collective-permute-start.13 = (bf16[32,1,16,16]{0,3,2,1:T(8,128)(2,1)S(1)}, bf16[32,1,16,16]{0,3,2,1:T(8,128)(2,1)S(1)}, u32[]{:S(2)}, u32[]{:S(2)}) collective-permute-start(bf16[32,1,16,16]{0,3,2,1:T(8,128)(2,1)S(1)} %get-tuple-element.10), channel_id=1, source_target_pairs={{16,0},{32,16},{48,32},{64,48},{80,64},{96,80},{112,96},{128,112},... | collective-permute-start | bytes 49160 | tf_op jit(solution)/shard_map/ppermute | solution.py:19
  121.6 1.9 %collective-permute-done.13 = bf16[32,1,16,16]{0,3,2,1:T(8,128)(2,1)S(1)} collective-permute-done((bf16[32,1,16,16]{0,3,2,1:T(8,128)(2,1)S(1)}, bf16[32,1,16,16]{0,3,2,1:T(8,128)(2,1)S(1)}, u32[]{:S(2)}, u32[]{:S(2)}) %collective-permute-start.13) | collective-permute-done | bytes 16416 | tf_op jit(solution)/shard_map/ppermute | solution.py:19
  123.5 1.9 %collective-permute-start.14 = (bf16[32,18,1,16]{0,3,2,1:T(8,128)(2,1)S(1)}, bf16[32,18,1,16]{0,3,2,1:T(8,128)(2,1)S(1)}, u32[]{:S(2)}, u32[]{:S(2)}) collective-permute-start(bf16[32,18,1,16]{0,3,2,1:T(8,128)(2,1)S(1)} %get-tuple-element.5), channel_id=1, source_target_pairs={{0,1},{1,2},{2,3},{3,4},{4,5},{5,6},{6,7},{7,8},{8,9},{9,10},{10,1... | collective-permute-start | bytes 55304 | tf_op jit(solution)/shard_map/ppermute | solution.py:17
  125.4 4.1 %collective-permute-start.15 = (bf16[32,18,1,16]{0,3,2,1:T(8,128)(2,1)S(1)}, bf16[32,18,1,16]{0,3,2,1:T(8,128)(2,1)S(1)}, u32[]{:S(2)}, u32[]{:S(2)}) collective-permute-start(bf16[32,18,1,16]{0,3,2,1:T(8,128)(2,1)S(1)} %get-tuple-element.6), channel_id=1, source_target_pairs={{1,0},{2,1},{3,2},{4,3},{5,4},{6,5},{7,6},{8,7},{9,8},{10,9},{11,1... | collective-permute-start | bytes 55304 | tf_op jit(solution)/shard_map/ppermute | solution.py:19
  129.8 7.9 %collective-permute-done.15 = bf16[32,18,1,16]{0,3,2,1:T(8,128)(2,1)S(1)} collective-permute-done((bf16[32,18,1,16]{0,3,2,1:T(8,128)(2,1)S(1)}, bf16[32,18,1,16]{0,3,2,1:T(8,128)(2,1)S(1)}, u32[]{:S(2)}, u32[]{:S(2)}) %collective-permute-start.15) | collective-permute-done | bytes 18464 | tf_op jit(solution)/shard_map/ppermute | solution.py:19
  137.7 1.7 %fusion.18 = bf16[32,18,18,1,18]{0,4,2,1,3:T(8,128)(2,1)S(1)} fusion(bf16[32,18,1,16]{0,3,2,1:T(8,128)(2,1)S(1)} %collective-permute-done.15, bf16[32,18,1,16]{0,3,2,1:T(8,128)(2,1)S(1)} %collective-permute-done.14, bf16[32,1,16,16]{0,3,2,1:T(8,128)(2,1)S(1)} %collective-permute-done.13, bf16[32,16,16,16]{0,3,2,1:T(8,128)(2,1)S(1)} %multiply_convert_fusion.1, ...), kind=kLoop, calls=%fused_computation.26 | loop fusion | flops 3359232 | bytes 705024 | tf_op jit(solution)/shard_map/broadcast_in_dim | solution.py:32
  139.5 1.7 %pad.21 = bf16[32,18,18,1,24]{0,4,2,1,3:T(8,128)(2,1)} pad(bf16[32,18,18,1,18]{0,4,2,1,3:T(8,128)(2,1)S(1)} %fusion.18, bf16[]{:T(256)} %constant.3.clone.1), padding=0_0x0_0x0_0x0_0x0_6 | pad | bytes 870914 | tf_op jit(solution)/shard_map/broadcast_in_dim | solution.py:32
  141.2 5.1 %reshape.55 = bf16[32,18,18,1,8,3]{0,5,4,2,1,3:T(4,128)(2,1)S(1)} reshape(bf16[32,18,18,1,24]{0,4,2,1,3:T(8,128)(2,1)} %pad.21) | data formatting | bytes 995328 | tf_op jit(solution)/shard_map/conv_general_dilated | solution.py:31
  147.0 0.6 copy-done.4
  147.6 4.4 %select_convert_fusion = bf16[16,16,8,3,32]{4,2,3,1,0:T(8,128)(2,1)S(1)} fusion(bf16[3,3,3,32,32]{4,3,2,1,0:T(8,128)(2,1)S(1)} %copy-done.4, bf16[32,18,18,1,7,2]{0,4,5,2,1,3:T(8,128)(2,1)S(1)} %slice.83, bf16[32,18,18,1,8,3]{0,4,5,2,1,3:T(8,128)(2,1)S(1)} %copy.25, pred[8,3]{0,1:T(4,128)(4,1)S(1)} %copy-done.10), kind=kOutput, calls=%fused_computation.19 | convolution fusion | flops 342620160 | bytes 1236504 | tf_op jit(solution)/shard_map/conv_general_dilated | solution.py:31
  152.9 1.2 copy.28
  (51 shorter events, 4.9 us)
Async XLA Ops:
  0.0 24.4 %copy-start.7 = (bf16[27,1024]{1,0:T(8,128)(2,1)S(1)}, bf16[27,1024]{1,0:T(8,128)(2,1)}, u32[]{:S(2)}) copy-start(bf16[27,1024]{1,0:T(8,128)(2,1)} %param.8) | copy-start | bytes 165892
  0.0 25.3 %copy-start.8 = (bf16[8,2048]{1,0:T(8,128)(2,1)S(1)}, bf16[8,2048]{1,0:T(8,128)(2,1)}, u32[]{:S(2)}) copy-start(bf16[8,2048]{1,0:T(8,128)(2,1)} %param.9) | copy-start | bytes 98308
  1.5 9.5 %collective-permute-start = (bf16[32,1,16,16]{0,3,2,1:T(8,128)(2,1)S(1)}, bf16[32,1,16,16]{0,3,2,1:T(8,128)(2,1)S(1)}, u32[]{:S(2)}, u32[]{:S(2)}) collective-permute-start(bf16[32,1,16,16]{0,3,2,1:T(8,128)(2,1)S(1)} %get-tuple-element.11), channel_id=1, source_target_pairs={{0,16},{16,32},{32,48},{48,64},{64,80},{80,96},{96,112},{112,128},... | collective-permute-start | bytes 49160 | tf_op jit(solution)/shard_map/ppermute | solution.py:17
  3.5 9.5 %collective-permute-start.1 = (bf16[32,1,16,16]{0,3,2,1:T(8,128)(2,1)S(1)}, bf16[32,1,16,16]{0,3,2,1:T(8,128)(2,1)S(1)}, u32[]{:S(2)}, u32[]{:S(2)}) collective-permute-start(bf16[32,1,16,16]{0,3,2,1:T(8,128)(2,1)S(1)} %get-tuple-element.12), channel_id=1, source_target_pairs={{16,0},{32,16},{48,32},{64,48},{80,64},{96,80},{112,96},{128,112},... | collective-permute-start | bytes 49160 | tf_op jit(solution)/shard_map/ppermute | solution.py:19
  13.0 12.5 %collective-permute-start.2 = (bf16[32,18,1,16]{0,3,2,1:T(8,128)(2,1)S(1)}, bf16[32,18,1,16]{0,3,2,1:T(8,128)(2,1)S(1)}, u32[]{:S(2)}, u32[]{:S(2)}) collective-permute-start(bf16[32,18,1,16]{0,3,2,1:T(8,128)(2,1)S(1)} %get-tuple-element.7), channel_id=1, source_target_pairs={{0,1},{1,2},{2,3},{3,4},{4,5},{5,6},{6,7},{7,8},{8,9},{9,10},{10,1... | collective-permute-start | bytes 55304 | tf_op jit(solution)/shard_map/ppermute | solution.py:17
  21.9 12.3 %collective-permute-start.3 = (bf16[32,18,1,16]{0,3,2,1:T(8,128)(2,1)S(1)}, bf16[32,18,1,16]{0,3,2,1:T(8,128)(2,1)S(1)}, u32[]{:S(2)}, u32[]{:S(2)}) collective-permute-start(bf16[32,18,1,16]{0,3,2,1:T(8,128)(2,1)S(1)} %get-tuple-element.8), channel_id=1, source_target_pairs={{1,0},{2,1},{3,2},{4,3},{5,4},{6,5},{7,6},{8,7},{9,8},{10,9},{11,1... | collective-permute-start | bytes 55304 | tf_op jit(solution)/shard_map/ppermute | solution.py:19
  25.5 24.8 %copy-start = (bf16[2,2,2,64,32]{4,3,2,1,0:T(8,128)(2,1)}, bf16[2,2,2,64,32]{4,3,2,1,0:T(8,128)(2,1)S(1)}, u32[]{:S(2)}) copy-start(bf16[2,2,2,64,32]{4,3,2,1,0:T(8,128)(2,1)S(1)} %reshape.35) | copy-start | bytes 98308
  43.1 0.9 copy-start.3
  43.1 0.9 copy-start.9
  50.1 17.1 %copy-start.5 = (bf16[64,8,64]{2,1,0:T(8,128)(2,1)S(1)}, bf16[64,8,64]{2,1,0:T(8,128)(2,1)}, u32[]{:S(2)}) copy-start(bf16[64,8,64]{2,1,0:T(8,128)(2,1)} %param.11) | copy-start | bytes 196612
  50.9 8.3 %collective-permute-start.4 = (bf16[64,1,8,8]{0,3,2,1:T(8,128)(2,1)S(1)}, bf16[64,1,8,8]{0,3,2,1:T(8,128)(2,1)S(1)}, u32[]{:S(2)}, u32[]{:S(2)}) collective-permute-start(bf16[64,1,8,8]{0,3,2,1:T(8,128)(2,1)S(1)} %get-tuple-element.19), channel_id=1, source_target_pairs={{0,16},{16,32},{32,48},{48,64},{64,80},{80,96},{96,112},{112,128},... | collective-permute-start | bytes 24584 | tf_op jit(solution)/shard_map/ppermute | solution.py:17
  52.8 7.8 %collective-permute-start.5 = (bf16[64,1,8,8]{0,3,2,1:T(8,128)(2,1)S(1)}, bf16[64,1,8,8]{0,3,2,1:T(8,128)(2,1)S(1)}, u32[]{:S(2)}, u32[]{:S(2)}) collective-permute-start(bf16[64,1,8,8]{0,3,2,1:T(8,128)(2,1)S(1)} %get-tuple-element.20), channel_id=1, source_target_pairs={{16,0},{32,16},{48,32},{64,48},{80,64},{96,80},{112,96},{128,112},... | collective-permute-start | bytes 24584 | tf_op jit(solution)/shard_map/ppermute | solution.py:19
  60.6 7.4 %copy-start.6 = (bf16[64,1,8,8]{0,3,2,1:T(8,128)(2,1)}, bf16[64,1,8,8]{0,3,2,1:T(8,128)(2,1)S(1)}, u32[]{:S(2)}) copy-start(bf16[64,1,8,8]{0,3,2,1:T(8,128)(2,1)S(1)} %collective-permute-done.5) | copy-start | bytes 24580
  61.2 10.0 %collective-permute-start.6 = (bf16[64,10,1,8]{0,3,2,1:T(8,128)(2,1)}, bf16[64,10,1,8]{0,3,2,1:T(8,128)(2,1)}, u32[]{:S(2)}, u32[]{:S(2)}) collective-permute-start(bf16[64,10,1,8]{0,3,2,1:T(8,128)(2,1)} %get-tuple-element.15), channel_id=1, source_target_pairs={{0,1},{1,2},{2,3},{3,4},{4,5},{5,6},{6,7},{7,8},{8,9},{9,10},{10,1... | collective-permute-start | bytes 30728 | tf_op jit(solution)/shard_map/ppermute | solution.py:17
  63.1 12.0 %collective-permute-start.7 = (bf16[64,10,1,8]{0,3,2,1:T(8,128)(2,1)}, bf16[64,10,1,8]{0,3,2,1:T(8,128)(2,1)}, u32[]{:S(2)}, u32[]{:S(2)}) collective-permute-start(bf16[64,10,1,8]{0,3,2,1:T(8,128)(2,1)} %get-tuple-element.16), channel_id=1, source_target_pairs={{1,0},{2,1},{3,2},{4,3},{5,4},{6,5},{7,6},{8,7},{9,8},{10,9},{11,1... | collective-permute-start | bytes 30728 | tf_op jit(solution)/shard_map/ppermute | solution.py:19
  82.8 8.3 %collective-permute-start.8 = (bf16[64,1,8,8]{0,3,2,1:T(8,128)(2,1)S(1)}, bf16[64,1,8,8]{0,3,2,1:T(8,128)(2,1)S(1)}, u32[]{:S(2)}, u32[]{:S(2)}) collective-permute-start(bf16[64,1,8,8]{0,3,2,1:T(8,128)(2,1)S(1)} %get-tuple-element.17), channel_id=1, source_target_pairs={{0,16},{16,32},{32,48},{48,64},{64,80},{80,96},{96,112},{112,128},... | collective-permute-start | bytes 24584 | tf_op jit(solution)/shard_map/ppermute | solution.py:17
  84.7 7.8 %collective-permute-start.9 = (bf16[64,1,8,8]{0,3,2,1:T(8,128)(2,1)S(1)}, bf16[64,1,8,8]{0,3,2,1:T(8,128)(2,1)S(1)}, u32[]{:S(2)}, u32[]{:S(2)}) collective-permute-start(bf16[64,1,8,8]{0,3,2,1:T(8,128)(2,1)S(1)} %get-tuple-element.18), channel_id=1, source_target_pairs={{16,0},{32,16},{48,32},{64,48},{80,64},{96,80},{112,96},{128,112},... | collective-permute-start | bytes 24584 | tf_op jit(solution)/shard_map/ppermute | solution.py:19
  92.5 6.8 %collective-permute-start.10 = (bf16[64,10,1,8]{0,3,2,1:T(8,128)(2,1)S(1)}, bf16[64,10,1,8]{0,3,2,1:T(8,128)(2,1)S(1)}, u32[]{:S(2)}, u32[]{:S(2)}) collective-permute-start(bf16[64,10,1,8]{0,3,2,1:T(8,128)(2,1)S(1)} %get-tuple-element.13), channel_id=1, source_target_pairs={{0,1},{1,2},{2,3},{3,4},{4,5},{5,6},{6,7},{7,8},{8,9},{9,10},{10,1... | collective-permute-start | bytes 30728 | tf_op jit(solution)/shard_map/ppermute | solution.py:17
  96.6 11.7 %collective-permute-start.11 = (bf16[64,10,1,8]{0,3,2,1:T(8,128)(2,1)S(1)}, bf16[64,10,1,8]{0,3,2,1:T(8,128)(2,1)S(1)}, u32[]{:S(2)}, u32[]{:S(2)}) collective-permute-start(bf16[64,10,1,8]{0,3,2,1:T(8,128)(2,1)S(1)} %get-tuple-element.14), channel_id=1, source_target_pairs={{1,0},{2,1},{3,2},{4,3},{5,4},{6,5},{7,6},{8,7},{9,8},{10,9},{11,1... | collective-permute-start | bytes 30728 | tf_op jit(solution)/shard_map/ppermute | solution.py:19
  99.1 9.4 %copy-start.2 = (bf16[3,3,3,64,64]{4,3,2,1,0:T(8,128)(2,1)S(1)}, bf16[3,3,3,64,64]{4,3,2,1,0:T(8,128)(2,1)}, u32[]{:S(2)}) copy-start(bf16[3,3,3,64,64]{4,3,2,1,0:T(8,128)(2,1)} %reshape.36) | copy-start | bytes 663556
  108.5 2.0 %copy-start.1 = (bf16[2,2,2,64,32]{4,3,2,1,0:T(8,128)(2,1)S(1)}, bf16[2,2,2,64,32]{4,3,2,1,0:T(8,128)(2,1)}, u32[]{:S(2)}) copy-start(bf16[2,2,2,64,32]{4,3,2,1,0:T(8,128)(2,1)} %copy-done) | copy-start | bytes 98308
  113.3 8.3 %collective-permute-start.12 = (bf16[32,1,16,16]{0,3,2,1:T(8,128)(2,1)S(1)}, bf16[32,1,16,16]{0,3,2,1:T(8,128)(2,1)S(1)}, u32[]{:S(2)}, u32[]{:S(2)}) collective-permute-start(bf16[32,1,16,16]{0,3,2,1:T(8,128)(2,1)S(1)} %get-tuple-element.9), channel_id=1, source_target_pairs={{0,16},{16,32},{32,48},{48,64},{64,80},{80,96},{96,112},{112,128},... | collective-permute-start | bytes 49160 | tf_op jit(solution)/shard_map/ppermute | solution.py:17
  115.2 8.2 %collective-permute-start.13 = (bf16[32,1,16,16]{0,3,2,1:T(8,128)(2,1)S(1)}, bf16[32,1,16,16]{0,3,2,1:T(8,128)(2,1)S(1)}, u32[]{:S(2)}, u32[]{:S(2)}) collective-permute-start(bf16[32,1,16,16]{0,3,2,1:T(8,128)(2,1)S(1)} %get-tuple-element.10), channel_id=1, source_target_pairs={{16,0},{32,16},{48,32},{64,48},{80,64},{96,80},{112,96},{128,112},... | collective-permute-start | bytes 49160 | tf_op jit(solution)/shard_map/ppermute | solution.py:19
  123.5 6.2 %collective-permute-start.14 = (bf16[32,18,1,16]{0,3,2,1:T(8,128)(2,1)S(1)}, bf16[32,18,1,16]{0,3,2,1:T(8,128)(2,1)S(1)}, u32[]{:S(2)}, u32[]{:S(2)}) collective-permute-start(bf16[32,18,1,16]{0,3,2,1:T(8,128)(2,1)S(1)} %get-tuple-element.5), channel_id=1, source_target_pairs={{0,1},{1,2},{2,3},{3,4},{4,5},{5,6},{6,7},{7,8},{8,9},{9,10},{10,1... | collective-permute-start | bytes 55304 | tf_op jit(solution)/shard_map/ppermute | solution.py:17
  125.4 12.3 %collective-permute-start.15 = (bf16[32,18,1,16]{0,3,2,1:T(8,128)(2,1)S(1)}, bf16[32,18,1,16]{0,3,2,1:T(8,128)(2,1)S(1)}, u32[]{:S(2)}, u32[]{:S(2)}) collective-permute-start(bf16[32,18,1,16]{0,3,2,1:T(8,128)(2,1)S(1)} %get-tuple-element.6), channel_id=1, source_target_pairs={{1,0},{2,1},{3,2},{4,3},{5,4},{6,5},{7,6},{8,7},{9,8},{10,9},{11,1... | collective-permute-start | bytes 55304 | tf_op jit(solution)/shard_map/ppermute | solution.py:19
  146.6 0.9 copy-start.4
  146.7 0.9 copy-start.10
where the time goes:
time: 155 us; the launch traced here: 154 us
  starting transfers between devices  63.2 us (41%)
  waiting for transfers between devices  36.2 us (23%)
  local copies, waits for them, and re-layouts  27.2 us (18%)
  matrix products  18.9 us (12%)
  other arithmetic  7.4 us (5%)
    ppermute x8, starting transfers between devices, extended(): lax.ppermute(head, axis, [((i + 1) % count, i) for i in range(ends)])  38.7 us
    ppermute x8, waiting for transfers between devices, extended(): lax.ppermute(head, axis, [((i + 1) % count, i) for i in range(ends)])  36 us
    ppermute x8, starting transfers between devices, extended(): lax.ppermute(tail, axis, [(i, (i + 1) % count) for i in range(ends)])  24.4 us
    conv_general_dilated x4, matrix products, conv_local(): lax.conv_general_dilated(padded[None], kernel, (1, 1, 1), 'VALID', dimens...  17.9 us
    conv_general_dilated x8, local copies, waits for them, and re-layouts, conv_local(): lax.conv_general_dilated(padded[None], kernel, (1, 1, 1), 'VALID', dimens...  12.3 us
    broadcast_in_dim x4, other arithmetic, conv_local(): padded[None]  4.71 us
    broadcast_in_dim x2, local copies, waits for them, and re-layouts, conv_local(): padded[None]  3.48 us
    reshape x3, local copies, waits for them, and re-layouts, unpack_kernel(): kernel.reshape(side, side, side, size_out, size_in).transpose(3, 4, 0, 1, 2)  3.2 us
  transfers between devices with their start and end apart: 16, of which 9 were waited for; matrix products, arithmetic and copies ran while one was open for 4% of the time, Pallas kernels for 0%

commit v1 on v0

v1 whole, which is shorter than its diff:
```python
import jax
import jax.numpy as jnp
from jax import lax
from jax.experimental import pallas as pl
from jax.experimental.pallas import tpu as pltpu
from jax.sharding import PartitionSpec as P

C1 = 32
C2 = 64
LANES = 256
HALO = 4
NB = 8
WIDE = NB + 2 * HALO
YMSG = NB * HALO * NB + 32 + 16
XMSG = 192 + 48 + 16 + 64
F32 = jnp.float32
BF16 = jnp.bfloat16
NT = (((1,), (1,)), ((), ()))
TN = (((0,), (0,)), ((), ()))


def iota(shape, dim):
    return lax.broadcasted_iota(jnp.int32, shape, dim)


def one_hot(cond):
    return jnp.where(cond, 1.0, 0.0).astype(BF16)


def dot(a, b):
    return jnp.dot(a, b, preferred_element_type=F32)


def block_sum_matrix():
    r, l = iota((64, 256), 0), iota((64, 256), 1)
    return one_hot((r // 8 == l // 32) & (r % 8 == (l % 16) // 2))


def parity_matrix():
    r, l = iota((256, 256), 0), iota((256, 256), 1)
    return one_hot(((r // 64) % 2 == (l // 16) % 2) & ((r // 32) % 2 == l % 2))


def is_odd(axis):
    return lax.rem(lax.axis_index(axis), 2)


def pack_kernel(flag_ref, feat_ref, own_ref, first_ref, second_ref, f_scr):
    odd = is_odd("gy")
    marks = jnp.full((16, LANES), flag_ref[0].astype(F32), F32).astype(BF16)
    q = block_sum_matrix()
    parity = parity_matrix()
    cells = feat_ref[...].astype(F32).reshape(512, 256)
    f_scr[0] = cells[:, :128]
    f_scr[1] = cells[:, 128:]
    for xb in range(NB):
        parts = []
        for a0 in range(2):
            at = pl.ds(2 * xb + a0, C1, stride=16)
            rows = jnp.concatenate([f_scr[0, at, :], f_scr[1, at, :]], axis=1).astype(BF16)
            parts += [rows] * 4
        spread = jnp.concatenate(parts, axis=0) * parity
        own_ref[xb] = lax.dot_general(q, spread, NT, preferred_element_type=F32).astype(BF16)
    for ref, side in ((first_ref, odd), (second_ref, 1 - odd)):
        for xb in range(NB):
            ref[pl.ds(xb * 32, 32), :] = own_ref[xb, pl.ds(pl.multiple_of(32 * side, 32), 32), :]
        ref[pl.ds(288, 16), :] = marks


def pack_cot_kernel(flag_ref, cot_ref, first_in, second_in, cown_ref, first_ref, second_ref, c_scr):
    odd = is_odd("gy")
    for ref, features in ((first_ref, first_in), (second_ref, second_in)):
        ref[pl.ds(0, 256), :] = features[pl.ds(0, 256), :]
        ref[pl.ds(288, 16), :] = features[pl.ds(288, 16), :]
    eye = one_hot(iota((64, 64), 0) == iota((64, 64), 1))
    c_scr[:, :64] = cot_ref[...].astype(F32).reshape(512, 64) * flag_ref[0].astype(F32)
    for p in range(4):
        rows = jnp.concatenate(
            [c_scr[pl.ds(2 * p + b, C2, stride=8), :] for b in range(2)], axis=0
        )[:, :64].astype(BF16)
        cown_ref[p] = lax.dot_general(eye, rows, NT, preferred_element_type=F32).astype(BF16)
    for ref, side in ((first_ref, odd), (second_ref, 1 - odd)):
        for p in range(4):
            at = (pl.ds(256 + 16 * (p // 2), 16), pl.ds(128 * (p % 2), 128))
            ref[at] = cown_ref[p, pl.ds(pl.multiple_of(48 * side, 16), 16), :]


OFFSETS = {(0, 0): 0, (1, 0): 1, (0, 1): 2, (1, 1): -1}


def fine_weights(u_ref, out_ref, u_scr, v_scr, w_scr, backward):
    tile = one_hot(iota((32, 256), 0) == iota((32, 256), 1) % 32)
    u_scr[...] = dot(u_ref[...], tile).astype(BF16).reshape(27, 32, 256)
    lane = iota((32, 256), 1)
    low2 = one_hot((lane // 32) % 2 == 0), one_hot((lane // 32) % 2 == 1)
    low1 = one_hot((lane // 64) % 2 == 0), one_hot((lane // 64) % 2 == 1)

    def taps(f):
        return ((-f, 1 - f) if backward else (f, f - 1))

    def mix(load, f, masks):
        terms = [load(e) * mask for e, mask in zip(taps(f), masks) if abs(e) <= 1]
        return sum(terms[1:], terms[0])

    def body(e0, carry):
        for e1 in range(3):
            for f2 in range(-1, 3):
                v_scr[e0 * 12 + e1 * 4 + (f2 + 1)] = mix(
                    lambda e2: u_scr[e0 * 9 + e1 * 3 + e2 + 1], f2, low2
                )
        for f1 in range(-1, 3):
            for f2 in range(-1, 3):
                w_scr[e0 * 16 + (f1 + 1) * 4 + f2 + 1] = mix(
                    lambda e1: v_scr[e0 * 12 + (e1 + 1) * 4 + f2 + 1], f1, low1
                )
        return carry

    lax.fori_loop(0, 3, body, 0)
    half = jnp.zeros((32, 128), BF16)
    for my in range(2):
        for mz in range(2):
            for mx in range(2):
                for a0 in range(2):
                    for a1 in range(2):
                        for a2 in range(2):
                            f0, f1, f2 = OFFSETS[a0, mx], OFFSETS[a1, my], OFFSETS[a2, mz]
                            row = ((my * 2 + mz) * 2 + mx) * 256 + (a0 * 4 + a1 * 2 + a2) * 32
                            for b0, e0 in enumerate(taps(f0)):
                                at = (pl.ds(row, 32), pl.ds(128 * b0, 128))
                                if abs(e0) <= 1:
                                    out_ref[at] = w_scr[(e0 + 1) * 16 + (f1 + 1) * 4 + f2 + 1, :, 128 * b0 : 128 * b0 + 128]
                                else:
                                    out_ref[at] = half


def coarse_weights(u_ref, out_ref, u_scr, backward):
    if backward:
        tile = one_hot(iota((64, 128), 0) == iota((64, 128), 1) % 64)
        u_scr[...] = dot(u_ref[...], tile).astype(BF16).reshape(27, 64, 128)
    else:
        eye = one_hot(iota((64, 64), 0) == iota((64, 64), 1))
        for e in range(27):
            turned = lax.dot_general(eye, u_ref[pl.ds(64 * e, 64), :], NT, preferred_element_type=F32)
            u_scr[e] = jnp.concatenate([turned, turned], axis=1).astype(BF16)
    masks = one_hot(iota((64, 128), 1) < 64), one_hot(iota((64, 128), 1) >= 64)

    def body(t, carry):
        k = 8 - t if backward else t
        for s in range(4):
            taps = (1 - s, 2 - s) if backward else (s - 1, s - 2)
            terms = [u_scr[(e + 1) * 9 + k] * mask for e, mask in zip(taps, masks) if abs(e) <= 1]
            out_ref[pl.ds(t * 256 + s * 64, 64), :] = sum(terms[1:], terms[0])
        return carry

    lax.fori_loop(0, 9, body, 0)


def weight_kernel(
    u1_ref, u1b_ref, u2_ref, kd_ref, ku_ref,
    w1_ref, w2_ref, w3_ref, w4_ref, wd_ref, wu_ref,
    u_scr, v_scr, w_scr, uc_scr,
):
    fine_weights(u1_ref, w1_ref, u_scr, v_scr, w_scr, False)
    fine_weights(u1b_ref, w2_ref, u_scr, v_scr, w_scr, True)
    coarse_weights(u2_ref, w3_ref, uc_scr, False)
    coarse_weights(u2_ref, w4_ref, uc_scr, True)
    for b in range(2):
        place = one_hot(iota((64, 128), 0) + 64 * b == iota((64, 128), 1))
        wd_ref[pl.ds(256 * b, 256), :] = dot(kd_ref[...], place).astype(BF16)
        zero = jnp.zeros((64, 256), BF16)
        wu_ref[b, pl.ds(64 * b, 64), :] = ku_ref[...]
        wu_ref[b, pl.ds(64 * (1 - b), 64), :] = zero


def silu_parts(v):
    s = 0.5 + 0.5 * jnp.tanh(0.5 * v)
    vs = v * s
    return vs, s + vs * (1.0 - s)


def shift_z(cells, up):
    z = iota(cells.shape, 1)
    if up:
        return jnp.where(z < 7, pltpu.roll(cells, 7, 1), 0.0)
    return jnp.where(z > 0, pltpu.roll(cells, 1, 1), 0.0)


def mixed(cells, store):
    n = cells.shape[0]
    rows = (n - 2) * 8
    lane = iota(cells.shape, 2)
    zmix = jnp.where((lane // 32) % 2 == 0, shift_z(cells, True), shift_z(cells, False))
    low1 = (iota((n - 2, 8, 256), 2) // 64) % 2 == 0
    for mz, form in enumerate((cells, zmix)):
        store(mz, form[1 : n - 1].reshape(rows, 256).astype(BF16))
        store(2 + mz, jnp.where(low1, form[2:], form[: n - 2]).reshape(rows, 256).astype(BF16))


def conv_lhs(before, here, after):
    parts = []
    for m in range(4):
        parts += [here[0][m, here[1]], after[0][m, after[1], :, :128], before[0][m, before[1], :, 128:]]
    return jnp.concatenate(parts, axis=1)


def coarse_forms(cells, store):
    n = cells.shape[0]
    for dz, form in enumerate((shift_z(cells, False), cells, shift_z(cells, True))):
        for dy in range(3):
            store(dy * 3 + dz, form[dy : dy + n - 2].reshape((n - 2) * 8, 128).astype(BF16))


def storer(scr, slot):
    def store(m, value):
        scr[m, slot] = value

    return store


def pair_lhs(low, high):
    parts = []
    for t in range(9):
        parts += [low[0][t, low[1]], high[0][t, high[1]]]
    return jnp.concatenate(parts, axis=1)


def spread_block(p_scr, slot, cells):
    mixed(cells.astype(F32).reshape(16, 8, 256), storer(p_scr, slot))


def forward_pair(places, marks, w1_ref, wd_ref, dv_scr, dv_slot, d_scr, d_slot):
    lhs = jnp.concatenate([conv_lhs(*places[:3]), conv_lhs(*places[1:])], axis=0)
    pre = dot(lhs, w1_ref[...])
    hidden = []
    for b in range(2):
        value, slope = silu_parts(pre[112 * b : 112 * b + 112])
        flags = jnp.concatenate([marks(b)] * 2, axis=1)
        hidden.append((flags * value).astype(BF16))
        dv_scr[dv_slot + b] = (flags * slope)[16:96]
    down = dot(jnp.concatenate(hidden, axis=1), wd_ref[...]).astype(BF16)
    coarse_forms(down.astype(F32).reshape(14, 8, 128), storer(d_scr, d_slot))
    return down


def coarse_forward(places, cots, w3_ref, g_scr, g_first):
    lhs = jnp.concatenate([pair_lhs(*places[:2]), pair_lhs(*places[1:])], axis=0)
    pre = dot(lhs, w3_ref[...])
    for k in range(2):
        _, slope = silu_parts(pre[96 * k : 96 * k + 96])
        grad = (cots(k).astype(F32) * slope).astype(BF16)
        coarse_forms(grad.astype(F32).reshape(12, 8, 128), storer(g_scr, g_first + k))


def fine_gradient(grad, slopes, wu_ref, q_scr, slot):
    for b in range(2):
        fine = (dot(grad, wu_ref[b]) * slopes(b)).astype(BF16)
        mixed(fine.astype(F32).reshape(10, 8, 256), storer(q_scr, slot + b))


def edge_kernel(
    flag_ref, own_ref, cown_ref, ya_ref, yb_ref, w1_ref, wd_ref,
    first_ref, second_ref, cot_ref, marks_ref, p_ref, dv_ref, d_ref,
    ext_ref, down_scr,
):
    odd_y, odd_x = is_odd("gy"), is_odd("gx")

    def place(above, below):
        for xb in range(NB):
            ext_ref[xb, pl.ds(0, 32), :] = above[pl.ds(xb * 32, 32), :]
            ext_ref[xb, pl.ds(32, 64), :] = own_ref[xb]
            ext_ref[xb, pl.ds(96, 32), :] = below[pl.ds(xb * 32, 32), :]
        for p in range(4):
            at = (pl.ds(256 + 16 * (p // 2), 16), pl.ds(128 * (p % 2), 128))
            cot_ref[p, pl.ds(0, 16), :] = above[at]
            cot_ref[p, pl.ds(16, 64), :] = cown_ref[p]
            cot_ref[p, pl.ds(80, 16), :] = below[at]
        for k in range(2):
            marks_ref[pl.ds(16 * k, 16), :] = above[pl.ds(288, 16), pl.ds(0, 128)]
            marks_ref[pl.ds(96 + 16 * k, 16), :] = below[pl.ds(288, 16), pl.ds(0, 128)]

    marks_ref[pl.ds(32, 64), :] = jnp.full((64, 128), flag_ref[0].astype(F32), F32).astype(BF16)
    pl.when(odd_y == 1)(lambda: place(yb_ref, ya_ref))
    pl.when(odd_y == 0)(lambda: place(ya_ref, yb_ref))

    marks = marks_ref[...].astype(F32)[8:120]
    for k in range(NB):
        spread_block(p_ref, k, ext_ref[k])
    for n in range(2):
        places = [(p_ref, 4 * n + k) for k in range(4)]
        down_scr[n] = forward_pair(places, lambda b: marks, w1_ref, wd_ref, dv_ref, 2 * n, d_ref, n)

    def send(low, high):
        for ref, n, near, outer, lane in ((low, 0, 0, 1, 0), (high, 1, 7, 6, 128)):
            ref[pl.ds(0, 128), :] = ext_ref[near]
            for h in range(2):
                half = pl.ds(128 * h, 128)
                ref[pl.ds(128, 64), half] = ext_ref[outer, pl.ds(64 * h, 64), pl.ds(lane, 128)]
                ref[pl.ds(192, 48), half] = cot_ref[3 * n, pl.ds(48 * h, 48), :]
            ends = [marks_ref[pl.ds(96 * k, 16), :].astype(F32)[:8] for k in range(2)]
            ref[pl.ds(240, 16), pl.ds(0, 128)] = jnp.concatenate(ends, axis=0).astype(BF16)
            ref[pl.ds(240, 16), pl.ds(128, 128)] = marks_ref[pl.ds(32, 16), :]
            ref[pl.ds(256, 64), pl.ds(0, 128)] = down_scr[n, pl.ds(0, 64), :]
            ref[pl.ds(256, 48), pl.ds(128, 128)] = down_scr[n, pl.ds(64, 48), :]
            ref[pl.ds(304, 16), pl.ds(128, 128)] = jnp.zeros((16, 128), BF16)

    pl.when(odd_x == 1)(lambda: send(second_ref, first_ref))
    pl.when(odd_x == 0)(lambda: send(first_ref, second_ref))


def middle_kernel(
    cot_ref, marks_ref, p_ref, d_ref, w1_ref, w3_ref, w4_ref, wd_ref, wu_ref,
    g_ref, q_ref,
    dv_scr, d_scr,
):
    marks = marks_ref[...].astype(F32)[8:120]
    places = [(p_ref, 2 + k) for k in range(4)]
    forward_pair(places, lambda b: marks, w1_ref, wd_ref, dv_scr, 0, d_scr, 0)
    places = [(d_ref, 0), (d_scr, 0), (d_ref, 1)]
    coarse_forward(places, lambda k: cot_ref[1 + k], w3_ref, g_ref, 0)
    grad = dot(pair_lhs((g_ref, 0), (g_ref, 1)), w4_ref[...]).astype(BF16)
    fine_gradient(grad, lambda b: dv_scr[b], wu_ref, q_ref, 0)


def main_kernel(
    cot_ref, marks_ref, xa_ref, xb_ref, pe_ref, dve_ref, de_ref, gm_ref, qm_ref,
    w1_ref, w2_ref, w3_ref, w4_ref, wd_ref, wu_ref,
    out_ref,
    p_scr, flag_scr, dv_scr, d_scr, cot_scr, g_scr, q_scr, o_scr,
):
    odd = is_odd("gx")

    def receive(left_ref, right_ref):
        sides = ((left_ref, 0, 0, 0, 1, 0, 128), (right_ref, 2, 3, 3, 2, 3, 0))
        for ref, flag_slot, cot_slot, d_slot, near, outer, lane in sides:
            ends = ref[pl.ds(240, 16), pl.ds(0, 128)].astype(F32)
            own = ref[pl.ds(240, 16), pl.ds(128, 128)].astype(F32)
            flag_scr[flag_slot] = jnp.concatenate([ends[:8]] * 3 + [own] * 4 + [ends[8:]] * 3, axis=0)
            for h in range(2):
                cot_scr[cot_slot, pl.ds(48 * h, 48), :] = ref[pl.ds(192, 48), pl.ds(128 * h, 128)]
            down = [ref[pl.ds(256, 64 - 16 * h), pl.ds(128 * h, 128)] for h in range(2)]
            down = jnp.concatenate(down, axis=0).astype(F32)
            coarse_forms(down.reshape(14, 8, 128), storer(d_scr, d_slot))
            spread_block(p_scr, near, ref[pl.ds(0, 128), :])
            half = jnp.concatenate([ref[pl.ds(128, 64), pl.ds(128 * h, 128)] for h in range(2)], axis=0)
            zero = jnp.zeros((128, 128), BF16)
            spread_block(p_scr, outer, jnp.concatenate([half, zero] if lane == 0 else [zero, half], axis=1))

    pl.when(odd == 1)(lambda: receive(xb_ref, xa_ref))
    pl.when(odd == 0)(lambda: receive(xa_ref, xb_ref))
    flag_scr[1] = marks_ref[...].astype(F32)[8:120]
    cot_scr[1] = cot_ref[0]
    cot_scr[2] = cot_ref[3]
    for m in range(4):
        for k in range(2):
            q_scr[m, 4 + k] = qm_ref[m, k]

    left = [(p_scr, 0), (p_scr, 1), (pe_ref, 0), (pe_ref, 1)]
    right = [(pe_ref, 6), (pe_ref, 7), (p_scr, 2), (p_scr, 3)]
    for n, (places, regions) in enumerate(((left, (0, 1)), (right, (1, 2)))):
        forward_pair(places, lambda b: flag_scr[regions[b]], w1_ref, wd_ref, dv_scr, 2 * n, d_scr, 1 + n)

    coarse_forward([(d_scr, 0), (d_scr, 1), (de_ref, 0)], lambda k: cot_scr[k], w3_ref, g_scr, 0)
    coarse_forward([(de_ref, 1), (d_scr, 2), (d_scr, 3)], lambda k: cot_scr[2 + k], w3_ref, g_scr, 2)

    left = [(g_scr, 0), (g_scr, 1), (gm_ref, 0)]
    right = [(gm_ref, 1), (g_scr, 2), (g_scr, 3)]
    slopes = [((dv_scr, 0), (dve_ref, 0)), ((dve_ref, 2), (dv_scr, 2))]
    for n, places in enumerate((left, right)):
        lhs = jnp.concatenate([pair_lhs(*places[:2]), pair_lhs(*places[1:])], axis=0)
        grad = dot(lhs, w4_ref[...]).astype(BF16)
        for k in range(2):
            ref, slot = slopes[n][k]
            fine_gradient(grad[80 * k : 80 * k + 80], lambda b: ref[slot + b], wu_ref, q_scr, 6 * n + 2 * k)

    q = block_sum_matrix()
    parity = parity_matrix().astype(F32)
    for h in range(2):
        lhs = jnp.concatenate(
            [conv_lhs(*((q_scr, 4 * h + k + n) for n in range(3))) for k in range(4)], axis=0
        )
        grad = dot(lhs, w2_ref[...]).astype(BF16)
        for k in range(4):
            spread = lax.dot_general(grad[64 * k : 64 * k + 64], q, TN, preferred_element_type=F32) * parity
            for b in range(2):
                rows = sum(spread[128 * b + 32 * i : 128 * b + 32 * i + 32] for i in range(4))
                at = pl.ds(8 * h + 2 * k + b, C1, stride=16)
                o_scr[0, at, :] = rows[:, :128]
                o_scr[1, at, :] = rows[:, 128:]
    cells = jnp.concatenate([o_scr[0], o_scr[1]], axis=1)
    out_ref[...] = cells.reshape(32, 16, 256).astype(BF16)


VMEM = pl.BlockSpec(memory_space=pltpu.VMEM)
SMEM = pl.BlockSpec(memory_space=pltpu.SMEM)


def call(kernel, specs, outs, scratch, flops, nbytes, *args):
    return pl.pallas_call(
        kernel,
        out_shape=outs,
        in_specs=specs,
        out_specs=jax.tree.map(lambda _: VMEM, outs),
        scratch_shapes=scratch,
        compiler_params=pltpu.CompilerParams(vmem_limit_bytes=24 * 1024 * 1024),
        cost_estimate=pl.CostEstimate(flops=flops, bytes_accessed=nbytes, transcendentals=0),
    )(*args)


def shape(*dims, dtype=BF16):
    return jax.ShapeDtypeStruct(dims, dtype)


def swaps(first, second, axis):
    count = lax.axis_size(axis)

    def both_ways(start):
        edges = [(i, i + 1) for i in range(start, count - 1, 2)]
        return edges + [(j, i) for i, j in edges]

    return lax.ppermute(first, axis, both_ways(1)), lax.ppermute(second, axis, both_ways(0))


def on_device(features, brick_mask, kernel_fine, kernel_down, kernel_coarse, cotangent):
    flag = brick_mask.reshape(1)
    own, y_first, y_second = call(
        pack_kernel,
        [SMEM, VMEM],
        [shape(8, 64, 256), shape(YMSG, 256), shape(YMSG, 256)],
        [pltpu.VMEM((2, 512, 128), F32)],
        2 * 10**9, 10**6, flag, features,
    )
    cown, y_first, y_second = call(
        pack_cot_kernel,
        [SMEM, VMEM, VMEM, VMEM],
        [shape(4, 64, 128), shape(YMSG, 256), shape(YMSG, 256)],
        [pltpu.VMEM((512, 128), F32)],
        10**9, 10**5, flag, cotangent, y_first, y_second,
    )
    y_a, y_b = swaps(y_first, y_second, "gy")
    fine = kernel_fine.reshape(27, C1, C1)
    down = kernel_down.reshape(8, C2, C1)
    w1, w2, w3, w4, wd, wu = call(
        weight_kernel,
        [VMEM] * 5,
        [shape(2048, 256), shape(2048, 256), shape(2304, 128), shape(2304, 128), shape(512, 128), shape(2, 128, 256)],
        [
            pltpu.VMEM((27, 32, 256), BF16),
            pltpu.VMEM((36, 32, 256), BF16),
            pltpu.VMEM((48, 32, 256), BF16),
            pltpu.VMEM((27, 64, 128), BF16),
        ],
        10**9, 10**7,
        fine.transpose(0, 2, 1).reshape(27 * C1, C1),
        fine.reshape(27 * C1, C1),
        kernel_coarse.reshape(27 * C2, C2),
        down.transpose(0, 2, 1).reshape(8 * C1, C2),
        down.transpose(1, 0, 2).reshape(C2, 8 * C1),
    )
    x_first, x_second, cot, marks, pe, dve, de = call(
        edge_kernel,
        [SMEM] + [VMEM] * 6,
        [
            shape(XMSG, 256), shape(XMSG, 256), shape(4, 96, 128), shape(128, 128),
            shape(4, 8, 112, 256), shape(4, 80, 256, dtype=F32), shape(9, 2, 96, 128),
        ],
        [pltpu.VMEM((8, 128, 256), BF16), pltpu.VMEM((2, 112, 128), BF16)],
        5 * 10**8, 10**6, flag, own, cown, y_a, y_b, w1, wd,
    )
    x_a, x_b = swaps(x_first, x_second, "gx")
    gm, qm = call(
        middle_kernel,
        [VMEM] * 9,
        [shape(9, 2, 80, 128), shape(4, 2, 64, 256)],
        [pltpu.VMEM((2, 80, 256), F32), pltpu.VMEM((9, 1, 96, 128), BF16)],
        5 * 10**9, 10**7,
        cot, marks, pe, de, w1, w3, w4, wd, wu,
    )
    return call(
        main_kernel,
        [VMEM] * 15,
        shape(32, 16, 256),
        [
            pltpu.VMEM((4, 4, 112, 256), BF16),
            pltpu.VMEM((3, 112, 128), F32),
            pltpu.VMEM((4, 80, 256), F32),
            pltpu.VMEM((9, 4, 96, 128), BF16),
            pltpu.VMEM((4, 96, 128), BF16),
            pltpu.VMEM((9, 4, 80, 128), BF16),
            pltpu.VMEM((4, 10, 64, 256), BF16),
            pltpu.VMEM((2, 512, 128), F32),
        ],
        10**10, 10**7,
        cot, marks, x_a, x_b, pe, dve, de, gm, qm, w1, w2, w3, w4, wd, wu,
    )


def solution(mesh):
    placed = (P(None, "gx", "gy"), P("gx", "gy", None), P(), P(), P(), P(None, "gx", "gy"))
    return jax.shard_map(
        on_device, mesh=mesh, in_specs=placed, out_specs=P(None, "gx", "gy"), check_vma=False
    )
```

time: 155 us -> 38 us (0.25)
  starting transfers between devices: 63.2 us -> 17.7 us
  waiting for transfers between devices: 36.2 us -> 4.66 us
  local copies, waits for them, and re-layouts: 27.2 us -> 2.76 us
  matrix products: 18.9 us -> 0 us
  Pallas kernels: 0 us -> 11.8 us
  other arithmetic: 7.4 us -> 0 us
    ppermute x16 -> x4, starting transfers between devices: 63.2 us -> 17.7 us  [the longest x2 13.8 us: swaps(): lax.ppermute(first, axis, both_ways(1))]
    ppermute x16 -> x4, waiting for transfers between devices: 36.2 us -> 4.66 us  [the longest x2 3.63 us: swaps(): lax.ppermute(first, axis, both_ways(1))]
    conv_general_dilated x5 -> x0, matrix products: 18.5 us -> none  [the longest x4 17.9 us: conv_local(): lax.conv_general_dilated(padded[None], kernel, (1, 1, 1), 'VALID', dimens...]
    conv_general_dilated x8 -> x0, local copies, waits for them, and re-layouts: 12.3 us -> none  [conv_local(): lax.conv_general_dilated(padded[None], kernel, (1, 1, 1), 'VALID', dimens...]
    pallas_call x0 -> x6, Pallas kernels: none -> 11.8 us  [call(): pl.pallas_call(kernel, out_shape=outs, in_specs=specs, out_specs=jax.tree...]
    broadcast_in_dim x4 -> x0, other arithmetic: 4.71 us -> none  [conv_local(): padded[None]]
    broadcast_in_dim x2 -> x0, local copies, waits for them, and re-layouts: 3.48 us -> none  [conv_local(): padded[None]]
    convert_element_type x8 -> x0, local copies, waits for them, and re-layouts: 3.27 us -> none  [the longest x4 2.06 us: on_device(): conv_local(depth_pad(grad_rim_fine), flipped(kernel_fine))]
  transfers between devices with their start and end apart: 16 -> 4, of which waited for: 9 -> 3; matrix products, arithmetic and copies ran while one was open for 4% -> 4% of each run, Pallas kernels for 0% -> 11%
where the time goes in v1:
time: 38 us; the launch traced here: 37.7 us
  starting transfers between devices  17.7 us (47%)
  Pallas kernels  11.8 us (31%)
  waiting for transfers between devices  4.66 us (12%)
  local copies, waits for them, and re-layouts  2.76 us (7%)
  between operations  0.81 us (2%)
    ppermute x2, starting transfers between devices, swaps(): lax.ppermute(first, axis, both_ways(1))  13.8 us
    pallas_call x6, Pallas kernels, call(): pl.pallas_call(kernel, out_shape=outs, in_specs=specs, out_specs=jax.tree...  11.8 us
    ppermute x2, starting transfers between devices, swaps(): lax.ppermute(second, axis, both_ways(0))  3.84 us
    ppermute x2, waiting for transfers between devices, swaps(): lax.ppermute(first, axis, both_ways(1))  3.63 us
    unnamed x10, local copies, waits for them, and re-layouts  1.34 us
    ppermute x2, waiting for transfers between devices, swaps(): lax.ppermute(second, axis, both_ways(0))  1.03 us
  transfers between devices with their start and end apart: 4, of which 3 were waited for; matrix products, arithmetic and copies ran while one was open for 4% of the time, Pallas kernels for 11%

profile of v1, /device:TPU:62, one launch (start us, length us, event | category | flops | bytes accessed | tf_op | source)
XLA Modules:
  0.0 37.7 jit_solution(18442809279710453786)
XLA Ops:
  0.7 0.0 copy-start
  0.7 0.9 %copy-done = bf16[32,16,256]{2,1,0:T(8,128)(2,1)S(1)} copy-done((bf16[32,16,256]{2,1,0:T(8,128)(2,1)S(1)}, bf16[32,16,256]{2,1,0:T(8,128)(2,1)}, u32[]{:S(2)}) %copy-start) | copy-done | bytes 262168
  1.6 0.0 copy-start.1
  1.6 0.5 %shard_map.64 = (bf16[8,64,256]{2,1,0:T(8,128)(2,1)S(1)}, bf16[304,256]{1,0:T(8,128)(2,1)S(1)}, bf16[304,256]{1,0:T(8,128)(2,1)S(1)}) custom-call(s32[1]{0:T(128)} %bitcast.8.flag_ref, bf16[32,16,256]{2,1,0:T(8,128)(2,1)S(1)} %copy-done), custom_call_target="tpu_custom_call" | custom-call | flops 2000000000 | bytes 1000000 | tf_op jit(solution)/shard_map/pallas_call | solution.py:398
  2.1 0.4 %copy-done.1 = bf16[64,8,64]{2,1,0:T(8,128)(2,1)S(1)} copy-done((bf16[64,8,64]{2,1,0:T(8,128)(2,1)S(1)}, bf16[64,8,64]{2,1,0:T(8,128)(2,1)}, u32[]{:S(2)}) %copy-start.1) | copy-done | bytes 65560
  2.5 0.0 copy-start.3
  2.5 0.0 copy-start.4
  2.5 0.0 copy-start.2
  2.5 0.2 shard_map.65
  2.8 10.1 %collective-permute-start = (bf16[304,256]{1,0:T(8,128)(2,1)S(1)}, bf16[304,256]{1,0:T(8,128)(2,1)S(1)}, u32[]{:S(2)}, u32[]{:S(2)}) collective-permute-start(bf16[304,256]{1,0:T(8,128)(2,1)S(1)} %get-tuple-element.30), channel_id=1, source_target_pairs={{1,2},{3,4},{5,6},{7,8},{9,10},{11,12},{13,14},{2,1},{4,3},{6,5},{... | collective-permute-start | bytes 466952 | tf_op jit(solution)/shard_map/ppermute | solution.py:420
  12.9 1.9 %collective-permute-start.1 = (bf16[304,256]{1,0:T(8,128)(2,1)S(1)}, bf16[304,256]{1,0:T(8,128)(2,1)S(1)}, u32[]{:S(2)}, u32[]{:S(2)}) collective-permute-start(bf16[304,256]{1,0:T(8,128)(2,1)S(1)} %get-tuple-element.31), channel_id=1, source_target_pairs={{0,1},{2,3},{4,5},{6,7},{8,9},{10,11},{12,13},{14,15},{1,0},{3,2},... | collective-permute-start | bytes 466952 | tf_op jit(solution)/shard_map/ppermute | solution.py:420
  14.8 0.0 copy-done.3
  14.8 0.2 reshape_reshape.3.u1b_ref
  15.0 0.2 reshape.22
  15.2 0.0 copy-done.4
  15.2 0.1 reshape.25
  15.4 0.1 copy.11
  15.5 0.1 copy.12
  15.6 0.1 copy.13.ku_ref
  15.7 0.2 copy.10
  15.8 0.0 copy-done.2
  15.9 0.4 %reshape.24.u2_ref = bf16[1728,64]{1,0:T(8,128)(2,1)S(1)} reshape(bf16[27,4096]{1,0:T(8,128)(2,1)S(1)} %copy-done.2) | data formatting | bytes 442368 | tf_op jit(solution)/shard_map/reshape | solution.py:455
  16.3 2.4 %shard_map.66 = (bf16[2048,256]{1,0:T(8,128)(2,1)S(1)}, bf16[2048,256]{1,0:T(8,128)(2,1)S(1)}, bf16[2304,128]{1,0:T(8,128)(2,1)S(1)}, bf16[2304,128]{1,0:T(8,128...) custom-call(bf16[864,32]{1,0:T(8,128)(2,1)S(1)} %bitcast.11, ...), custom_call_target="tpu_custom_call" | custom-call | flops 1000000000 | bytes 10000000 | tf_op jit(solution)/shard_map/pallas_call | solution.py:398
  18.7 0.5 %collective-permute-done.ya_ref = bf16[304,256]{1,0:T(8,128)(2,1)S(1)} collective-permute-done((bf16[304,256]{1,0:T(8,128)(2,1)S(1)}, bf16[304,256]{1,0:T(8,128)(2,1)S(1)}, u32[]{:S(2)}, u32[]{:S(2)}) %collective-permute-start) | collective-permute-done | bytes 155680 | tf_op jit(solution)/shard_map/ppermute | solution.py:420
  19.2 1.0 %collective-permute-done.1.yb_ref = bf16[304,256]{1,0:T(8,128)(2,1)S(1)} collective-permute-done((bf16[304,256]{1,0:T(8,128)(2,1)S(1)}, bf16[304,256]{1,0:T(8,128)(2,1)S(1)}, u32[]{:S(2)}, u32[]{:S(2)}) %collective-permute-start.1) | collective-permute-done | bytes 155680 | tf_op jit(solution)/shard_map/ppermute | solution.py:420
  20.3 1.6 %shard_map.67 = (bf16[320,256]{1,0:T(8,128)(2,1)S(1)}, bf16[320,256]{1,0:T(8,128)(2,1)S(1)}, bf16[4,96,128]{2,1,0:T(8,128)(2,1)S(1)}, bf16[128,128]{1,0:T(8,128)...) custom-call(s32[1]{0:T(128)} %bitcast.10.flag_ref, ...), custom_call_target="tpu_custom_call" | custom-call | flops 500000000 | bytes 1000000 | tf_op jit(solution)/shard_map/pallas_call | solution.py:398
  21.8 3.7 %collective-permute-start.2 = (bf16[320,256]{1,0:T(8,128)(2,1)S(1)}, bf16[320,256]{1,0:T(8,128)(2,1)S(1)}, u32[]{:S(2)}, u32[]{:S(2)}) collective-permute-start(bf16[320,256]{1,0:T(8,128)(2,1)S(1)} %get-tuple-element.36), channel_id=1, source_target_pairs={{16,32},{48,64},{80,96},{112,128},{144,160},{176,192},{208,224},{2... | collective-permute-start | bytes 491528 | tf_op jit(solution)/shard_map/ppermute | solution.py:420
  25.5 1.9 %collective-permute-start.3 = (bf16[320,256]{1,0:T(8,128)(2,1)S(1)}, bf16[320,256]{1,0:T(8,128)(2,1)S(1)}, u32[]{:S(2)}, u32[]{:S(2)}) collective-permute-start(bf16[320,256]{1,0:T(8,128)(2,1)S(1)} %get-tuple-element.37), channel_id=1, source_target_pairs={{0,16},{32,48},{64,80},{96,112},{128,144},{160,176},{192,208},{224... | collective-permute-start | bytes 491528 | tf_op jit(solution)/shard_map/ppermute | solution.py:420
  27.5 1.8 %shard_map.68 = (bf16[9,2,80,128]{3,2,1,0:T(8,128)(2,1)S(1)}, bf16[4,2,64,256]{3,2,1,0:T(8,128)(2,1)S(1)}) custom-call(bf16[4,96,128]{2,1,0:T(8,128)(2,1)S(1)} %get-tuple-element.34.cot_ref, bf16[128,128]{1,0:T(8,128)(2,1)S(1)} %get-tuple-element.35.marks_ref, bf16[4,8,112,256]{3,2,1,0:T(8,128)(2,1)S(1)} %get-tuple-element.38.p_ref.pe_ref, ...), custom_call_target="tpu_custom_call" | custom-call | flops 5000000000 | bytes 10000000 | tf_op jit(solution)/shard_map/pallas_call | solution.py:398
  29.2 3.1 %collective-permute-done.2.xa_ref = bf16[320,256]{1,0:T(8,128)(2,1)S(1)} collective-permute-done((bf16[320,256]{1,0:T(8,128)(2,1)S(1)}, bf16[320,256]{1,0:T(8,128)(2,1)S(1)}, u32[]{:S(2)}, u32[]{:S(2)}) %collective-permute-start.2) | collective-permute-done | bytes 163872 | tf_op jit(solution)/shard_map/ppermute | solution.py:420
  32.3 0.0 collective-permute-done.3.xb_ref
  32.3 5.4 %shard_map.69 = bf16[32,16,256]{2,1,0:T(8,128)(2,1)} custom-call(bf16[4,96,128]{2,1,0:T(8,128)(2,1)S(1)} %get-tuple-element.34.cot_ref, bf16[128,128]{1,0:T(8,128)(2,1)S(1)} %get-tuple-element.35.marks_ref, bf16[320,256]{1,0:T(8,128)(2,1)S(1)} %collective-permute-done.2.xa_ref, bf16[320,256]{1,0:T(8,128)(2,1)S(1)} %collective-permute-done.3.xb_ref, ...), custom_call_target="tpu_custom_call" | custom-call | flops 10000000000 | bytes 10000000 | tf_op jit(solution)/shard_map/pallas_call | solution.py:398
Async XLA Ops:
  0.7 1.0 %copy-start = (bf16[32,16,256]{2,1,0:T(8,128)(2,1)S(1)}, bf16[32,16,256]{2,1,0:T(8,128)(2,1)}, u32[]{:S(2)}) copy-start(bf16[32,16,256]{2,1,0:T(8,128)(2,1)} %feat_ref.1) | copy-start | bytes 786436
  1.6 0.9 %copy-start.1 = (bf16[64,8,64]{2,1,0:T(8,128)(2,1)S(1)}, bf16[64,8,64]{2,1,0:T(8,128)(2,1)}, u32[]{:S(2)}) copy-start(bf16[64,8,64]{2,1,0:T(8,128)(2,1)} %cot_ref.1) | copy-start | bytes 196612
  2.5 12.3 %copy-start.3 = (bf16[27,1024]{1,0:T(8,128)(2,1)S(1)}, bf16[27,1024]{1,0:T(8,128)(2,1)}, u32[]{:S(2)}) copy-start(bf16[27,1024]{1,0:T(8,128)(2,1)} %param.8) | copy-start | bytes 165892
  2.5 12.7 %copy-start.4 = (bf16[8,2048]{1,0:T(8,128)(2,1)S(1)}, bf16[8,2048]{1,0:T(8,128)(2,1)}, u32[]{:S(2)}) copy-start(bf16[8,2048]{1,0:T(8,128)(2,1)} %param.9) | copy-start | bytes 98308
  2.5 13.3 %copy-start.2 = (bf16[27,4096]{1,0:T(8,128)(2,1)S(1)}, bf16[27,4096]{1,0:T(8,128)(2,1)}, u32[]{:S(2)}) copy-start(bf16[27,4096]{1,0:T(8,128)(2,1)} %param.10) | copy-start | bytes 663556
  2.8 16.5 %collective-permute-start = (bf16[304,256]{1,0:T(8,128)(2,1)S(1)}, bf16[304,256]{1,0:T(8,128)(2,1)S(1)}, u32[]{:S(2)}, u32[]{:S(2)}) collective-permute-start(bf16[304,256]{1,0:T(8,128)(2,1)S(1)} %get-tuple-element.30), channel_id=1, source_target_pairs={{1,2},{3,4},{5,6},{7,8},{9,10},{11,12},{13,14},{2,1},{4,3},{6,5},{... | collective-permute-start | bytes 466952 | tf_op jit(solution)/shard_map/ppermute | solution.py:420
  12.9 7.4 %collective-permute-start.1 = (bf16[304,256]{1,0:T(8,128)(2,1)S(1)}, bf16[304,256]{1,0:T(8,128)(2,1)S(1)}, u32[]{:S(2)}, u32[]{:S(2)}) collective-permute-start(bf16[304,256]{1,0:T(8,128)(2,1)S(1)} %get-tuple-element.31), channel_id=1, source_target_pairs={{0,1},{2,3},{4,5},{6,7},{8,9},{10,11},{12,13},{14,15},{1,0},{3,2},... | collective-permute-start | bytes 466952 | tf_op jit(solution)/shard_map/ppermute | solution.py:420
  21.8 10.5 %collective-permute-start.2 = (bf16[320,256]{1,0:T(8,128)(2,1)S(1)}, bf16[320,256]{1,0:T(8,128)(2,1)S(1)}, u32[]{:S(2)}, u32[]{:S(2)}) collective-permute-start(bf16[320,256]{1,0:T(8,128)(2,1)S(1)} %get-tuple-element.36), channel_id=1, source_target_pairs={{16,32},{48,64},{80,96},{112,128},{144,160},{176,192},{208,224},{2... | collective-permute-start | bytes 491528 | tf_op jit(solution)/shard_map/ppermute | solution.py:420
  25.5 6.8 %collective-permute-start.3 = (bf16[320,256]{1,0:T(8,128)(2,1)S(1)}, bf16[320,256]{1,0:T(8,128)(2,1)S(1)}, u32[]{:S(2)}, u32[]{:S(2)}) collective-permute-start(bf16[320,256]{1,0:T(8,128)(2,1)S(1)} %get-tuple-element.37), channel_id=1, source_target_pairs={{0,16},{32,48},{64,80},{96,112},{128,144},{160,176},{192,208},{224... | collective-permute-start | bytes 491528 | tf_op jit(solution)/shard_map/ppermute | solution.py:420

commit v2 on v1

--- a/solution.py
+++ b/solution.py
@@ -11,8 +11,8 @@
 HALO = 4
 NB = 8
 WIDE = NB + 2 * HALO
-YMSG = NB * HALO * NB + 32 + 16
-XMSG = 192 + 48 + 16 + 64
+YMSG = 192 + 32 + 32 + 16
+XMSG = 192 + 48 + 64
 F32 = jnp.float32
 BF16 = jnp.bfloat16
 NT = (((1,), (1,)), ((), ()))
@@ -45,14 +45,24 @@
     return lax.rem(lax.axis_index(axis), 2)
 
 
-def pack_kernel(flag_ref, feat_ref, own_ref, first_ref, second_ref, f_scr):
+def constant_kernel(q_ref, parity_ref):
+    q_ref[...] = block_sum_matrix()
+    parity_ref[...] = parity_matrix()
+
+
+def low_y(shape):
+    return (iota(shape, len(shape) - 1) // 64) % 2 == 0
+
+
+def pack_kernel(flag_ref, feat_ref, cot_ref, q_ref, parity_ref, own_ref, cown_ref, first_ref, second_ref, f_scr, c_scr, m_scr):
     odd = is_odd("gy")
-    marks = jnp.full((16, LANES), flag_ref[0].astype(F32), F32).astype(BF16)
-    q = block_sum_matrix()
-    parity = parity_matrix()
+    flag = flag_ref[0].astype(F32)
     cells = feat_ref[...].astype(F32).reshape(512, 256)
     f_scr[0] = cells[:, :128]
     f_scr[1] = cells[:, 128:]
+    c_scr[:, :64] = cot_ref[...].astype(F32).reshape(512, 64) * flag
+    parity = parity_ref[...]
+    blocks = []
     for xb in range(NB):
         parts = []
         for a0 in range(2):
@@ -60,29 +70,32 @@
             rows = jnp.concatenate([f_scr[0, at, :], f_scr[1, at, :]], axis=1).astype(BF16)
             parts += [rows] * 4
         spread = jnp.concatenate(parts, axis=0) * parity
-        own_ref[xb] = lax.dot_general(q, spread, NT, preferred_element_type=F32).astype(BF16)
-    for ref, side in ((first_ref, odd), (second_ref, 1 - odd)):
-        for xb in range(NB):
-            ref[pl.ds(xb * 32, 32), :] = own_ref[xb, pl.ds(pl.multiple_of(32 * side, 32), 32), :]
-        ref[pl.ds(288, 16), :] = marks
-
-
-def pack_cot_kernel(flag_ref, cot_ref, first_in, second_in, cown_ref, first_ref, second_ref, c_scr):
-    odd = is_odd("gy")
-    for ref, features in ((first_ref, first_in), (second_ref, second_in)):
-        ref[pl.ds(0, 256), :] = features[pl.ds(0, 256), :]
-        ref[pl.ds(288, 16), :] = features[pl.ds(288, 16), :]
+        blocks.append(lax.dot_general(q_ref[...], spread, NT, preferred_element_type=F32))
+        own_ref[xb] = blocks[xb].astype(BF16)
+    for n, (inner, outer) in enumerate(((0, 24), (40, 32))):
+        for j in range(4):
+            rows = [blocks[2 * j + k][inner : inner + 24] for k in range(2)]
+            m_scr[n, pl.ds(48 * j, 48), :] = jnp.concatenate(rows, axis=0).astype(BF16)
+        rows = []
+        for k in range(4):
+            here, there = (blocks[k + i][outer : outer + 8] for i in (0, 4))
+            there = pltpu.roll(there, 64 if n == 0 else 192, 1)
+            low = low_y((8, 256))
+            rows.append(jnp.where(low, here, there) if n == 0 else jnp.where(low, there, here))
+        m_scr[n, pl.ds(192, 32), :] = jnp.concatenate(rows, axis=0).astype(BF16)
+        m_scr[n, pl.ds(256, 16), :] = jnp.full((16, LANES), flag, F32).astype(BF16)
     eye = one_hot(iota((64, 64), 0) == iota((64, 64), 1))
-    c_scr[:, :64] = cot_ref[...].astype(F32).reshape(512, 64) * flag_ref[0].astype(F32)
     for p in range(4):
         rows = jnp.concatenate(
             [c_scr[pl.ds(2 * p + b, C2, stride=8), :] for b in range(2)], axis=0
         )[:, :64].astype(BF16)
-        cown_ref[p] = lax.dot_general(eye, rows, NT, preferred_element_type=F32).astype(BF16)
-    for ref, side in ((first_ref, odd), (second_ref, 1 - odd)):
-        for p in range(4):
-            at = (pl.ds(256 + 16 * (p // 2), 16), pl.ds(128 * (p % 2), 128))
-            ref[at] = cown_ref[p, pl.ds(pl.multiple_of(48 * side, 16), 16), :]
+        cells = lax.dot_general(eye, rows, NT, preferred_element_type=F32).astype(BF16)
+        cown_ref[p] = cells
+        at = (pl.ds(224 + 16 * (p // 2), 16), pl.ds(128 * (p % 2), 128))
+        m_scr[(0, *at)] = cells[:16]
+        m_scr[(1, *at)] = cells[48:]
+    first_ref[...] = m_scr[odd]
+    second_ref[...] = m_scr[1 - odd]
 
 
 OFFSETS = {(0, 0): 0, (1, 0): 1, (0, 1): 2, (1, 1): -1}
@@ -266,17 +279,25 @@
 
     def place(above, below):
         for xb in range(NB):
-            ext_ref[xb, pl.ds(0, 32), :] = above[pl.ds(xb * 32, 32), :]
-            ext_ref[xb, pl.ds(32, 64), :] = own_ref[xb]
-            ext_ref[xb, pl.ds(96, 32), :] = below[pl.ds(xb * 32, 32), :]
+            at = 48 * (xb // 2), 24 * (xb % 2)
+            inner = [ref[pl.ds(at[0], 48), :].astype(F32)[at[1] : at[1] + 24] for ref in (above, below)]
+            at = 192 + 16 * ((xb % 4) // 2), 8 * (xb % 2)
+            outer = [ref[pl.ds(at[0], 16), :].astype(F32)[at[1] : at[1] + 8] for ref in (above, below)]
+            if xb >= 4:
+                outer = [pltpu.roll(outer[0], 64, 1), pltpu.roll(outer[1], 192, 1)]
+            ext_ref[xb, pl.ds(0, 8), :] = outer[0]
+            ext_ref[xb, pl.ds(8, 24), :] = inner[0]
+            ext_ref[xb, pl.ds(32, 64), :] = own_ref[xb].astype(F32)
+            ext_ref[xb, pl.ds(96, 24), :] = inner[1]
+            ext_ref[xb, pl.ds(120, 8), :] = outer[1]
         for p in range(4):
-            at = (pl.ds(256 + 16 * (p // 2), 16), pl.ds(128 * (p % 2), 128))
+            at = (pl.ds(224 + 16 * (p // 2), 16), pl.ds(128 * (p % 2), 128))
             cot_ref[p, pl.ds(0, 16), :] = above[at]
             cot_ref[p, pl.ds(16, 64), :] = cown_ref[p]
             cot_ref[p, pl.ds(80, 16), :] = below[at]
         for k in range(2):
-            marks_ref[pl.ds(16 * k, 16), :] = above[pl.ds(288, 16), pl.ds(0, 128)]
-            marks_ref[pl.ds(96 + 16 * k, 16), :] = below[pl.ds(288, 16), pl.ds(0, 128)]
+            marks_ref[pl.ds(16 * k, 16), :] = above[pl.ds(256, 16), pl.ds(0, 128)]
+            marks_ref[pl.ds(96 + 16 * k, 16), :] = below[pl.ds(256, 16), pl.ds(0, 128)]
 
     marks_ref[pl.ds(32, 64), :] = jnp.full((64, 128), flag_ref[0].astype(F32), F32).astype(BF16)
     pl.when(odd_y == 1)(lambda: place(yb_ref, ya_ref))
@@ -291,17 +312,17 @@
 
     def send(low, high):
         for ref, n, near, outer, lane in ((low, 0, 0, 1, 0), (high, 1, 7, 6, 128)):
-            ref[pl.ds(0, 128), :] = ext_ref[near]
+            ref[pl.ds(0, 128), :] = ext_ref[near].astype(BF16)
             for h in range(2):
                 half = pl.ds(128 * h, 128)
-                ref[pl.ds(128, 64), half] = ext_ref[outer, pl.ds(64 * h, 64), pl.ds(lane, 128)]
+                ref[pl.ds(128, 64), half] = ext_ref[outer, pl.ds(64 * h, 64), pl.ds(lane, 128)].astype(BF16)
                 ref[pl.ds(192, 48), half] = cot_ref[3 * n, pl.ds(48 * h, 48), :]
+            ref[pl.ds(240, 64), pl.ds(0, 128)] = down_scr[n, pl.ds(0, 64), :]
+            ref[pl.ds(240, 48), pl.ds(128, 128)] = down_scr[n, pl.ds(64, 48), :]
             ends = [marks_ref[pl.ds(96 * k, 16), :].astype(F32)[:8] for k in range(2)]
-            ref[pl.ds(240, 16), pl.ds(0, 128)] = jnp.concatenate(ends, axis=0).astype(BF16)
-            ref[pl.ds(240, 16), pl.ds(128, 128)] = marks_ref[pl.ds(32, 16), :]
-            ref[pl.ds(256, 64), pl.ds(0, 128)] = down_scr[n, pl.ds(0, 64), :]
-            ref[pl.ds(256, 48), pl.ds(128, 128)] = down_scr[n, pl.ds(64, 48), :]
-            ref[pl.ds(304, 16), pl.ds(128, 128)] = jnp.zeros((16, 128), BF16)
+            own = marks_ref[pl.ds(32, 16), :].astype(F32)
+            flags = jnp.where(low_y((16, 128)), jnp.concatenate(ends, axis=0), own)
+            ref[pl.ds(288, 16), pl.ds(128, 128)] = flags.astype(BF16)
 
     pl.when(odd_x == 1)(lambda: send(second_ref, first_ref))
     pl.when(odd_x == 0)(lambda: send(first_ref, second_ref))
@@ -332,12 +353,14 @@
     def receive(left_ref, right_ref):
         sides = ((left_ref, 0, 0, 0, 1, 0, 128), (right_ref, 2, 3, 3, 2, 3, 0))
         for ref, flag_slot, cot_slot, d_slot, near, outer, lane in sides:
-            ends = ref[pl.ds(240, 16), pl.ds(0, 128)].astype(F32)
-            own = ref[pl.ds(240, 16), pl.ds(128, 128)].astype(F32)
+            flags = ref[pl.ds(288, 16), pl.ds(128, 128)].astype(F32)
+            turned = pltpu.roll(flags, 64, 1)
+            ends = jnp.where(low_y((16, 128)), flags, turned)
+            own = jnp.where(low_y((16, 128)), turned, flags)
             flag_scr[flag_slot] = jnp.concatenate([ends[:8]] * 3 + [own] * 4 + [ends[8:]] * 3, axis=0)
             for h in range(2):
                 cot_scr[cot_slot, pl.ds(48 * h, 48), :] = ref[pl.ds(192, 48), pl.ds(128 * h, 128)]
-            down = [ref[pl.ds(256, 64 - 16 * h), pl.ds(128 * h, 128)] for h in range(2)]
+            down = [ref[pl.ds(240, 64 - 16 * h), pl.ds(128 * h, 128)] for h in range(2)]
             down = jnp.concatenate(down, axis=0).astype(F32)
             coarse_forms(down.reshape(14, 8, 128), storer(d_scr, d_slot))
             spread_block(p_scr, near, ref[pl.ds(0, 128), :])
@@ -422,19 +445,13 @@
 
 def on_device(features, brick_mask, kernel_fine, kernel_down, kernel_coarse, cotangent):
     flag = brick_mask.reshape(1)
-    own, y_first, y_second = call(
+    q, parity = call(constant_kernel, [], [shape(64, 256), shape(256, 256)], [], 4 * 10**9, 10**5)
+    own, cown, y_first, y_second = call(
         pack_kernel,
-        [SMEM, VMEM],
-        [shape(8, 64, 256), shape(YMSG, 256), shape(YMSG, 256)],
-        [pltpu.VMEM((2, 512, 128), F32)],
-        2 * 10**9, 10**6, flag, features,
-    )
-    cown, y_first, y_second = call(
-        pack_cot_kernel,
-        [SMEM, VMEM, VMEM, VMEM],
-        [shape(4, 64, 128), shape(YMSG, 256), shape(YMSG, 256)],
-        [pltpu.VMEM((512, 128), F32)],
-        10**9, 10**5, flag, cotangent, y_first, y_second,
+        [SMEM] + [VMEM] * 4,
+        [shape(8, 64, 256), shape(4, 64, 128), shape(YMSG, 256), shape(YMSG, 256)],
+        [pltpu.VMEM((2, 512, 128), F32), pltpu.VMEM((512, 128), F32), pltpu.VMEM((2, YMSG, 256), BF16)],
+        2 * 10**9, 10**6, flag, features, cotangent, q, parity,
     )
     y_a, y_b = swaps(y_first, y_second, "gy")
     fine = kernel_fine.reshape(27, C1, C1)
@@ -463,7 +480,7 @@
             shape(XMSG, 256), shape(XMSG, 256), shape(4, 96, 128), shape(128, 128),
             shape(4, 8, 112, 256), shape(4, 80, 256, dtype=F32), shape(9, 2, 96, 128),
         ],
-        [pltpu.VMEM((8, 128, 256), BF16), pltpu.VMEM((2, 112, 128), BF16)],
+        [pltpu.VMEM((8, 128, 256), F32), pltpu.VMEM((2, 112, 128), BF16)],
         5 * 10**8, 10**6, flag, own, cown, y_a, y_b, w1, wd,
     )
     x_a, x_b = swaps(x_first, x_second, "gx")

time: 38 us -> 36.4 us (0.958)
  local copies, waits for them, and re-layouts: 2.76 us -> 1.66 us
  waiting for transfers between devices: 4.66 us -> 4.13 us
    unnamed x10, local copies, waits for them, and re-layouts: 1.34 us -> 0.24 us
    ppermute x2, waiting for transfers between devices: 3.63 us -> 2.93 us  [swaps(): lax.ppermute(first, axis, both_ways(1))]
  transfers between devices with their start and end apart: 4 -> 4, of which waited for: 3 -> 2; matrix products, arithmetic and copies ran while one was open for 4% -> 4% of each run, Pallas kernels for 11% -> 11%
where the time goes in v2:
time: 36.4 us; the launch traced here: 36.2 us
  starting transfers between devices  17.8 us (49%)
  Pallas kernels  11.7 us (32%)
  waiting for transfers between devices  4.13 us (11%)
  local copies, waits for them, and re-layouts  1.66 us (5%)
  between operations  0.86 us (2%)
    ppermute x2, starting transfers between devices, swaps(): lax.ppermute(first, axis, both_ways(1))  14 us
    pallas_call x6, Pallas kernels, call(): pl.pallas_call(kernel, out_shape=outs, in_specs=specs, out_specs=jax.tree...  11.7 us
    ppermute x2, starting transfers between devices, swaps(): lax.ppermute(second, axis, both_ways(0))  3.84 us
    ppermute x2, waiting for transfers between devices, swaps(): lax.ppermute(first, axis, both_ways(1))  2.93 us
    ppermute x2, waiting for transfers between devices, swaps(): lax.ppermute(second, axis, both_ways(0))  1.2 us
  transfers between devices with their start and end apart: 4, of which 2 were waited for; matrix products, arithmetic and copies ran while one was open for 4% of the time, Pallas kernels for 11%

profile of v2, /device:TPU:62, one launch (start us, length us, event | category | flops | bytes accessed | tf_op | source)
XLA Modules:
  0.0 36.2 jit_solution(8587838485770354524)
XLA Ops:
  0.0 0.0 copy-start.1
  0.0 0.0 copy-start
  0.0 0.1 shard_map.64
  0.8 0.1 copy-done.1
  0.9 0.1 copy-done
  1.0 0.0 copy-start.3
  1.0 0.0 copy-start.4
  1.0 0.6 %shard_map.65 = (bf16[8,64,256]{2,1,0:T(8,128)(2,1)S(1)}, bf16[4,64,128]{2,1,0:T(8,128)(2,1)S(1)}, bf16[272,256]{1,0:T(8,128)(2,1)S(1)}, bf16[272,256]{1,0:T(8,128)(2,1)S(1)}) custom-call(s32[1]{0:T(128)} %bitcast.8.flag_ref, bf16[32,16,256]{2,1,0:T(8,128)(2,1)S(1)} %copy-done, bf16[64,8,64]{2,1,0:T(8,128)(2,1)S(1)} %copy-done.1, ...), custom_call_target="tpu_custom_call" | custom-call | flops 2000000000 | bytes 1000000 | tf_op jit(solution)/shard_map/pallas_call | solution.py:421
  1.6 0.0 copy-start.2
  1.6 10.2 %collective-permute-start = (bf16[272,256]{1,0:T(8,128)(2,1)S(1)}, bf16[272,256]{1,0:T(8,128)(2,1)S(1)}, u32[]{:S(2)}, u32[]{:S(2)}) collective-permute-start(bf16[272,256]{1,0:T(8,128)(2,1)S(1)} %get-tuple-element.30), channel_id=1, source_target_pairs={{1,2},{3,4},{5,6},{7,8},{9,10},{11,12},{13,14},{2,1},{4,3},{6,5},{... | collective-permute-start | bytes 417800 | tf_op jit(solution)/shard_map/ppermute | solution.py:443
  11.9 1.9 %collective-permute-start.1 = (bf16[272,256]{1,0:T(8,128)(2,1)S(1)}, bf16[272,256]{1,0:T(8,128)(2,1)S(1)}, u32[]{:S(2)}, u32[]{:S(2)}) collective-permute-start(bf16[272,256]{1,0:T(8,128)(2,1)S(1)} %get-tuple-element.31), channel_id=1, source_target_pairs={{0,1},{2,3},{4,5},{6,7},{8,9},{10,11},{12,13},{14,15},{1,0},{3,2},... | collective-permute-start | bytes 417800 | tf_op jit(solution)/shard_map/ppermute | solution.py:443
  13.8 0.0 copy-done.3
  13.8 0.2 reshape_reshape.3.u1b_ref
  14.0 0.2 reshape.22
  14.2 0.0 copy-done.4
  14.2 0.1 reshape.25
  14.3 0.1 copy.11
  14.5 0.1 copy.12
  14.6 0.1 copy.13.ku_ref
  14.7 0.2 copy.10
  14.8 0.0 copy-done.2
  14.9 0.4 %reshape.24.u2_ref = bf16[1728,64]{1,0:T(8,128)(2,1)S(1)} reshape(bf16[27,4096]{1,0:T(8,128)(2,1)S(1)} %copy-done.2) | data formatting | bytes 442368 | tf_op jit(solution)/shard_map/reshape | solution.py:472
  15.3 2.4 %shard_map.66 = (bf16[2048,256]{1,0:T(8,128)(2,1)S(1)}, bf16[2048,256]{1,0:T(8,128)(2,1)S(1)}, bf16[2304,128]{1,0:T(8,128)(2,1)S(1)}, bf16[2304,128]{1,0:T(8,128...) custom-call(bf16[864,32]{1,0:T(8,128)(2,1)S(1)} %bitcast.10, ...), custom_call_target="tpu_custom_call" | custom-call | flops 1000000000 | bytes 10000000 | tf_op jit(solution)/shard_map/pallas_call | solution.py:421
  17.7 0.0 collective-permute-done.ya_ref
  17.7 1.2 %collective-permute-done.1.yb_ref = bf16[272,256]{1,0:T(8,128)(2,1)S(1)} collective-permute-done((bf16[272,256]{1,0:T(8,128)(2,1)S(1)}, bf16[272,256]{1,0:T(8,128)(2,1)S(1)}, u32[]{:S(2)}, u32[]{:S(2)}) %collective-permute-start.1) | collective-permute-done | bytes 139296 | tf_op jit(solution)/shard_map/ppermute | solution.py:443
  18.9 1.5 %shard_map.67 = (bf16[304,256]{1,0:T(8,128)(2,1)S(1)}, bf16[304,256]{1,0:T(8,128)(2,1)S(1)}, bf16[4,96,128]{2,1,0:T(8,128)(2,1)S(1)}, bf16[128,128]{1,0:T(8,128)...) custom-call(s32[1]{0:T(128)} %bitcast.9.flag_ref, ...), custom_call_target="tpu_custom_call" | custom-call | flops 500000000 | bytes 1000000 | tf_op jit(solution)/shard_map/pallas_call | solution.py:421
  20.4 3.7 %collective-permute-start.2 = (bf16[304,256]{1,0:T(8,128)(2,1)S(1)}, bf16[304,256]{1,0:T(8,128)(2,1)S(1)}, u32[]{:S(2)}, u32[]{:S(2)}) collective-permute-start(bf16[304,256]{1,0:T(8,128)(2,1)S(1)} %get-tuple-element.36), channel_id=1, source_target_pairs={{16,32},{48,64},{80,96},{112,128},{144,160},{176,192},{208,224},{2... | collective-permute-start | bytes 466952 | tf_op jit(solution)/shard_map/ppermute | solution.py:443
  24.2 1.9 %collective-permute-start.3 = (bf16[304,256]{1,0:T(8,128)(2,1)S(1)}, bf16[304,256]{1,0:T(8,128)(2,1)S(1)}, u32[]{:S(2)}, u32[]{:S(2)}) collective-permute-start(bf16[304,256]{1,0:T(8,128)(2,1)S(1)} %get-tuple-element.37), channel_id=1, source_target_pairs={{0,16},{32,48},{64,80},{96,112},{128,144},{160,176},{192,208},{224... | collective-permute-start | bytes 466952 | tf_op jit(solution)/shard_map/ppermute | solution.py:443
  26.1 1.8 %shard_map.68 = (bf16[9,2,80,128]{3,2,1,0:T(8,128)(2,1)S(1)}, bf16[4,2,64,256]{3,2,1,0:T(8,128)(2,1)S(1)}) custom-call(bf16[4,96,128]{2,1,0:T(8,128)(2,1)S(1)} %get-tuple-element.34.cot_ref, bf16[128,128]{1,0:T(8,128)(2,1)S(1)} %get-tuple-element.35.marks_ref, bf16[4,8,112,256]{3,2,1,0:T(8,128)(2,1)S(1)} %get-tuple-element.38.p_ref.pe_ref, ...), custom_call_target="tpu_custom_call" | custom-call | flops 5000000000 | bytes 10000000 | tf_op jit(solution)/shard_map/pallas_call | solution.py:421
  27.9 2.9 %collective-permute-done.2.xa_ref = bf16[304,256]{1,0:T(8,128)(2,1)S(1)} collective-permute-done((bf16[304,256]{1,0:T(8,128)(2,1)S(1)}, bf16[304,256]{1,0:T(8,128)(2,1)S(1)}, u32[]{:S(2)}, u32[]{:S(2)}) %collective-permute-start.2) | collective-permute-done | bytes 155680 | tf_op jit(solution)/shard_map/ppermute | solution.py:443
  30.8 0.0 collective-permute-done.3.xb_ref
  30.8 5.4 %shard_map.69 = bf16[32,16,256]{2,1,0:T(8,128)(2,1)} custom-call(bf16[4,96,128]{2,1,0:T(8,128)(2,1)S(1)} %get-tuple-element.34.cot_ref, bf16[128,128]{1,0:T(8,128)(2,1)S(1)} %get-tuple-element.35.marks_ref, bf16[304,256]{1,0:T(8,128)(2,1)S(1)} %collective-permute-done.2.xa_ref, bf16[304,256]{1,0:T(8,128)(2,1)S(1)} %collective-permute-done.3.xb_ref, ...), custom_call_target="tpu_custom_call" | custom-call | flops 10000000000 | bytes 10000000 | tf_op jit(solution)/shard_map/pallas_call | solution.py:421
Async XLA Ops:
  0.0 0.9 %copy-start.1 = (bf16[64,8,64]{2,1,0:T(8,128)(2,1)S(1)}, bf16[64,8,64]{2,1,0:T(8,128)(2,1)}, u32[]{:S(2)}) copy-start(bf16[64,8,64]{2,1,0:T(8,128)(2,1)} %cot_ref.1) | copy-start | bytes 196612
  0.0 1.0 %copy-start = (bf16[32,16,256]{2,1,0:T(8,128)(2,1)S(1)}, bf16[32,16,256]{2,1,0:T(8,128)(2,1)}, u32[]{:S(2)}) copy-start(bf16[32,16,256]{2,1,0:T(8,128)(2,1)} %feat_ref.1) | copy-start | bytes 786436
  1.0 12.8 %copy-start.3 = (bf16[27,1024]{1,0:T(8,128)(2,1)S(1)}, bf16[27,1024]{1,0:T(8,128)(2,1)}, u32[]{:S(2)}) copy-start(bf16[27,1024]{1,0:T(8,128)(2,1)} %param.8) | copy-start | bytes 165892
  1.0 13.2 %copy-start.4 = (bf16[8,2048]{1,0:T(8,128)(2,1)S(1)}, bf16[8,2048]{1,0:T(8,128)(2,1)}, u32[]{:S(2)}) copy-start(bf16[8,2048]{1,0:T(8,128)(2,1)} %param.9) | copy-start | bytes 98308
  1.6 13.2 %copy-start.2 = (bf16[27,4096]{1,0:T(8,128)(2,1)S(1)}, bf16[27,4096]{1,0:T(8,128)(2,1)}, u32[]{:S(2)}) copy-start(bf16[27,4096]{1,0:T(8,128)(2,1)} %param.10) | copy-start | bytes 663556
  1.6 16.1 %collective-permute-start = (bf16[272,256]{1,0:T(8,128)(2,1)S(1)}, bf16[272,256]{1,0:T(8,128)(2,1)S(1)}, u32[]{:S(2)}, u32[]{:S(2)}) collective-permute-start(bf16[272,256]{1,0:T(8,128)(2,1)S(1)} %get-tuple-element.30), channel_id=1, source_target_pairs={{1,2},{3,4},{5,6},{7,8},{9,10},{11,12},{13,14},{2,1},{4,3},{6,5},{... | collective-permute-start | bytes 417800 | tf_op jit(solution)/shard_map/ppermute | solution.py:443
  11.9 7.0 %collective-permute-start.1 = (bf16[272,256]{1,0:T(8,128)(2,1)S(1)}, bf16[272,256]{1,0:T(8,128)(2,1)S(1)}, u32[]{:S(2)}, u32[]{:S(2)}) collective-permute-start(bf16[272,256]{1,0:T(8,128)(2,1)S(1)} %get-tuple-element.31), channel_id=1, source_target_pairs={{0,1},{2,3},{4,5},{6,7},{8,9},{10,11},{12,13},{14,15},{1,0},{3,2},... | collective-permute-start | bytes 417800 | tf_op jit(solution)/shard_map/ppermute | solution.py:443
  20.4 10.3 %collective-permute-start.2 = (bf16[304,256]{1,0:T(8,128)(2,1)S(1)}, bf16[304,256]{1,0:T(8,128)(2,1)S(1)}, u32[]{:S(2)}, u32[]{:S(2)}) collective-permute-start(bf16[304,256]{1,0:T(8,128)(2,1)S(1)} %get-tuple-element.36), channel_id=1, source_target_pairs={{16,32},{48,64},{80,96},{112,128},{144,160},{176,192},{208,224},{2... | collective-permute-start | bytes 466952 | tf_op jit(solution)/shard_map/ppermute | solution.py:443
  24.2 6.6 %collective-permute-start.3 = (bf16[304,256]{1,0:T(8,128)(2,1)S(1)}, bf16[304,256]{1,0:T(8,128)(2,1)S(1)}, u32[]{:S(2)}, u32[]{:S(2)}) collective-permute-start(bf16[304,256]{1,0:T(8,128)(2,1)S(1)} %get-tuple-element.37), channel_id=1, source_target_pairs={{0,16},{32,48},{64,80},{96,112},{128,144},{160,176},{192,208},{224... | collective-permute-start | bytes 466952 | tf_op jit(solution)/shard_map/ppermute | solution.py:443

commit v3 on v2

--- a/solution.py
+++ b/solution.py
@@ -342,77 +342,92 @@
     fine_gradient(grad, lambda b: dv_scr[b], wu_ref, q_ref, 0)
 
 
-def main_kernel(
-    cot_ref, marks_ref, xa_ref, xb_ref, pe_ref, dve_ref, de_ref, gm_ref, qm_ref,
+def side_steps(
+    side, msg_ref, cot_ref, marks_ref, pe_ref, dve_ref, de_ref, gm_ref, qm_ref, q_ref, parity_ref,
     w1_ref, w2_ref, w3_ref, w4_ref, wd_ref, wu_ref,
-    out_ref,
-    p_scr, flag_scr, dv_scr, d_scr, cot_scr, g_scr, q_scr, o_scr,
+    store_out, scratch,
 ):
-    odd = is_odd("gx")
-
-    def receive(left_ref, right_ref):
-        sides = ((left_ref, 0, 0, 0, 1, 0, 128), (right_ref, 2, 3, 3, 2, 3, 0))
-        for ref, flag_slot, cot_slot, d_slot, near, outer, lane in sides:
-            flags = ref[pl.ds(288, 16), pl.ds(128, 128)].astype(F32)
-            turned = pltpu.roll(flags, 64, 1)
-            ends = jnp.where(low_y((16, 128)), flags, turned)
-            own = jnp.where(low_y((16, 128)), turned, flags)
-            flag_scr[flag_slot] = jnp.concatenate([ends[:8]] * 3 + [own] * 4 + [ends[8:]] * 3, axis=0)
-            for h in range(2):
-                cot_scr[cot_slot, pl.ds(48 * h, 48), :] = ref[pl.ds(192, 48), pl.ds(128 * h, 128)]
-            down = [ref[pl.ds(240, 64 - 16 * h), pl.ds(128 * h, 128)] for h in range(2)]
-            down = jnp.concatenate(down, axis=0).astype(F32)
-            coarse_forms(down.reshape(14, 8, 128), storer(d_scr, d_slot))
-            spread_block(p_scr, near, ref[pl.ds(0, 128), :])
-            half = jnp.concatenate([ref[pl.ds(128, 64), pl.ds(128 * h, 128)] for h in range(2)], axis=0)
-            zero = jnp.zeros((128, 128), BF16)
-            spread_block(p_scr, outer, jnp.concatenate([half, zero] if lane == 0 else [zero, half], axis=1))
-
-    pl.when(odd == 1)(lambda: receive(xb_ref, xa_ref))
-    pl.when(odd == 0)(lambda: receive(xa_ref, xb_ref))
-    flag_scr[1] = marks_ref[...].astype(F32)[8:120]
-    cot_scr[1] = cot_ref[0]
-    cot_scr[2] = cot_ref[3]
+    p_scr, flag_scr, dv_scr, d_scr, cot_scr, g_scr, q_scr = scratch
+    other = 1 - side
+    right = side.astype(F32)
+
+    spread_block(p_scr, 1 + side, msg_ref[pl.ds(0, 128), :])
+    half = [msg_ref[pl.ds(128, 64), pl.ds(128 * h, 128)] for h in range(2)]
+    half = jnp.concatenate(half, axis=0).astype(F32)
+    spread_block(p_scr, 3 * side, jnp.concatenate([half * right, half * (1.0 - right)], axis=1))
+    for k in range(2):
+        for m in range(4):
+            p_scr[m, 2 * other + k] = pe_ref[m, 6 * side + k]
+        dv_scr[2 * other + k] = dve_ref[2 * side + k]
+    flags = msg_ref[pl.ds(288, 16), pl.ds(128, 128)].astype(F32)
+    turned = pltpu.roll(flags, 64, 1)
+    ends = jnp.where(low_y((16, 128)), flags, turned)
+    own = jnp.where(low_y((16, 128)), turned, flags)
+    flag_scr[side] = jnp.concatenate([ends[:8]] * 3 + [own] * 4 + [ends[8:]] * 3, axis=0)
+    flag_scr[other] = marks_ref[...].astype(F32)[8:120]
+    for h in range(2):
+        cot_scr[side, pl.ds(48 * h, 48), :] = msg_ref[pl.ds(192, 48), pl.ds(128 * h, 128)]
+    cot_scr[other] = cot_ref[3 * side]
+    down = [msg_ref[pl.ds(240, 64 - 16 * h), pl.ds(128 * h, 128)] for h in range(2)]
+    down = jnp.concatenate(down, axis=0).astype(F32)
+    coarse_forms(down.reshape(14, 8, 128), storer(d_scr, 2 * side))
+    for t in range(9):
+        d_scr[t, 2 * other] = de_ref[t, side]
+        g_scr[t, 2 * other] = gm_ref[t, side]
     for m in range(4):
         for k in range(2):
-            q_scr[m, 4 + k] = qm_ref[m, k]
-
-    left = [(p_scr, 0), (p_scr, 1), (pe_ref, 0), (pe_ref, 1)]
-    right = [(pe_ref, 6), (pe_ref, 7), (p_scr, 2), (p_scr, 3)]
-    for n, (places, regions) in enumerate(((left, (0, 1)), (right, (1, 2)))):
-        forward_pair(places, lambda b: flag_scr[regions[b]], w1_ref, wd_ref, dv_scr, 2 * n, d_scr, 1 + n)
-
-    coarse_forward([(d_scr, 0), (d_scr, 1), (de_ref, 0)], lambda k: cot_scr[k], w3_ref, g_scr, 0)
-    coarse_forward([(de_ref, 1), (d_scr, 2), (d_scr, 3)], lambda k: cot_scr[2 + k], w3_ref, g_scr, 2)
-
-    left = [(g_scr, 0), (g_scr, 1), (gm_ref, 0)]
-    right = [(gm_ref, 1), (g_scr, 2), (g_scr, 3)]
-    slopes = [((dv_scr, 0), (dve_ref, 0)), ((dve_ref, 2), (dv_scr, 2))]
-    for n, places in enumerate((left, right)):
-        lhs = jnp.concatenate([pair_lhs(*places[:2]), pair_lhs(*places[1:])], axis=0)
-        grad = dot(lhs, w4_ref[...]).astype(BF16)
-        for k in range(2):
-            ref, slot = slopes[n][k]
-            fine_gradient(grad[80 * k : 80 * k + 80], lambda b: ref[slot + b], wu_ref, q_scr, 6 * n + 2 * k)
-
-    q = block_sum_matrix()
-    parity = parity_matrix().astype(F32)
-    for h in range(2):
-        lhs = jnp.concatenate(
-            [conv_lhs(*((q_scr, 4 * h + k + n) for n in range(3))) for k in range(4)], axis=0
-        )
-        grad = dot(lhs, w2_ref[...]).astype(BF16)
-        for k in range(4):
-            spread = lax.dot_general(grad[64 * k : 64 * k + 64], q, TN, preferred_element_type=F32) * parity
-            for b in range(2):
-                rows = sum(spread[128 * b + 32 * i : 128 * b + 32 * i + 32] for i in range(4))
-                at = pl.ds(8 * h + 2 * k + b, C1, stride=16)
-                o_scr[0, at, :] = rows[:, :128]
-                o_scr[1, at, :] = rows[:, 128:]
-    cells = jnp.concatenate([o_scr[0], o_scr[1]], axis=1)
-    out_ref[...] = cells.reshape(32, 16, 256).astype(BF16)
-
-
+            q_scr[m, 4 * other + k] = qm_ref[m, k]
+
+    places = [(p_scr, k) for k in range(4)]
+    forward_pair(places, lambda b: flag_scr[b], w1_ref, wd_ref, dv_scr, 2 * side, d_scr, 1)
+    coarse_forward([(d_scr, k) for k in range(3)], lambda k: cot_scr[k], w3_ref, g_scr, side)
+    lhs = jnp.concatenate([pair_lhs((g_scr, k), (g_scr, k + 1)) for k in range(2)], axis=0)
+    grad = dot(lhs, w4_ref[...]).astype(BF16)
+    for k in range(2):
+        fine_gradient(grad[80 * k : 80 * k + 80], lambda b: dv_scr[2 * k + b], wu_ref, q_scr, 2 * side + 2 * k)
+    lhs = jnp.concatenate([conv_lhs(*((q_scr, k + n) for n in range(3))) for k in range(4)], axis=0)
+    grad = dot(lhs, w2_ref[...]).astype(BF16)
+    parity = parity_ref[...].astype(F32)
+    for k in range(4):
+        spread = lax.dot_general(grad[64 * k : 64 * k + 64], q_ref[...], TN, preferred_element_type=F32) * parity
+        for b in range(2):
+            rows = sum(spread[128 * b + 32 * i : 128 * b + 32 * i + 32] for i in range(4))
+            store_out(2 * k + b, rows)
+
+
+def near_kernel(msg_ref, *refs):
+    inputs, out_ref, scratch = refs[:15], refs[15], refs[16:]
+
+    def store_out(x, rows):
+        for h in range(2):
+            out_ref[h, pl.ds(x, C1, stride=8), :] = rows[:, 128 * h : 128 * h + 128]
+
+    side_steps(1 - is_odd("gx"), msg_ref, *inputs, store_out, scratch)
+
+
+def far_kernel(msg_ref, near_ref, *refs):
+    inputs, out_ref, scratch, o_scr = refs[:15], refs[15], refs[16:-1], refs[-1]
+    side = is_odd("gx")
+    o_scr[1 - side] = near_ref[...]
+
+    def store_out(x, rows):
+        for h in range(2):
+            o_scr[side, h, pl.ds(x, C1, stride=8), :] = rows[:, 128 * h : 128 * h + 128]
+
+    side_steps(side, msg_ref, *inputs, store_out, scratch)
+    halves = [jnp.concatenate([o_scr[n, h].reshape(32, 8, 128) for h in range(2)], axis=2) for n in range(2)]
+    out_ref[...] = jnp.concatenate(halves, axis=1).astype(BF16)
+
+
+SIDE_SCRATCH = [
+    pltpu.VMEM((4, 4, 112, 256), BF16),
+    pltpu.VMEM((2, 112, 128), F32),
+    pltpu.VMEM((4, 80, 256), F32),
+    pltpu.VMEM((9, 3, 96, 128), BF16),
+    pltpu.VMEM((2, 96, 128), BF16),
+    pltpu.VMEM((9, 3, 80, 128), BF16),
+    pltpu.VMEM((4, 6, 64, 256), BF16),
+]
 VMEM = pl.BlockSpec(memory_space=pltpu.VMEM)
 SMEM = pl.BlockSpec(memory_space=pltpu.SMEM)
 
@@ -489,25 +504,23 @@
         [VMEM] * 9,
         [shape(9, 2, 80, 128), shape(4, 2, 64, 256)],
         [pltpu.VMEM((2, 80, 256), F32), pltpu.VMEM((9, 1, 96, 128), BF16)],
-        5 * 10**9, 10**7,
+        2 * 10**10, 10**7,
         cot, marks, pe, de, w1, w3, w4, wd, wu,
     )
+    shared = (cot, marks, pe, dve, de, gm, qm, q, parity, w1, w2, w3, w4, wd, wu)
+    near = call(
+        near_kernel,
+        [VMEM] * 16,
+        shape(2, 256, 128, dtype=F32),
+        SIDE_SCRATCH,
+        2 * 10**10, 10**7, x_b, *shared,
+    )
     return call(
-        main_kernel,
-        [VMEM] * 15,
+        far_kernel,
+        [VMEM] * 17,
         shape(32, 16, 256),
-        [
-            pltpu.VMEM((4, 4, 112, 256), BF16),
-            pltpu.VMEM((3, 112, 128), F32),
-            pltpu.VMEM((4, 80, 256), F32),
-            pltpu.VMEM((9, 4, 96, 128), BF16),
-            pltpu.VMEM((4, 96, 128), BF16),
-            pltpu.VMEM((9, 4, 80, 128), BF16),
-            pltpu.VMEM((4, 10, 64, 256), BF16),
-            pltpu.VMEM((2, 512, 128), F32),
-        ],
-        10**10, 10**7,
-        cot, marks, x_a, x_b, pe, dve, de, gm, qm, w1, w2, w3, w4, wd, wu,
+        SIDE_SCRATCH + [pltpu.VMEM((2, 2, 256, 128), F32)],
+        10**10, 10**7, x_a, near, *shared,
     )
 
 

time: 36.4 us -> 35.5 us (0.975)
  the two profiles are of different devices: /device:TPU:62 before, /device:TPU:55 now
where the time goes in v3:
time: 35.5 us; the launch traced here: 35.3 us
  starting transfers between devices  19.8 us (56%)
  Pallas kernels  12.9 us (36%)
  local copies, waits for them, and re-layouts  1.66 us (5%)
  between operations  0.89 us (3%)
    pallas_call x7, Pallas kernels, call(): pl.pallas_call(kernel, out_shape=outs, in_specs=specs, out_specs=jax.tree...  12.9 us
    ppermute x2, starting transfers between devices, swaps(): lax.ppermute(second, axis, both_ways(0))  12.4 us
    ppermute x2, starting transfers between devices, swaps(): lax.ppermute(first, axis, both_ways(1))  7.34 us
  transfers between devices with their start and end apart: 4, of which 0 were waited for; matrix products, arithmetic and copies ran while one was open for 4% of the time, Pallas kernels for 20%

profile of v3, /device:TPU:55, one launch (start us, length us, event | category | flops | bytes accessed | tf_op | source)
XLA Modules:
  0.0 35.3 jit_solution(6269627051378340631)
XLA Ops:
  0.0 0.0 copy-start.1
  0.0 0.0 copy-start
  0.0 0.1 shard_map.64
  0.8 0.1 copy-done.1
  0.9 0.1 copy-done
  1.0 0.0 copy-start.3
  1.0 0.0 copy-start.4
  1.0 0.6 %shard_map.65 = (bf16[8,64,256]{2,1,0:T(8,128)(2,1)S(1)}, bf16[4,64,128]{2,1,0:T(8,128)(2,1)S(1)}, bf16[272,256]{1,0:T(8,128)(2,1)S(1)}, bf16[272,256]{1,0:T(8,128)(2,1)S(1)}) custom-call(s32[1]{0:T(128)} %bitcast.8.flag_ref, bf16[32,16,256]{2,1,0:T(8,128)(2,1)S(1)} %copy-done, bf16[64,8,64]{2,1,0:T(8,128)(2,1)S(1)} %copy-done.1, ...), custom_call_target="tpu_custom_call" | custom-call | flops 2000000000 | bytes 1000000 | tf_op jit(solution)/shard_map/pallas_call | solution.py:436
  1.6 0.0 copy-start.2
  1.6 3.1 %collective-permute-start = (bf16[272,256]{1,0:T(8,128)(2,1)S(1)}, bf16[272,256]{1,0:T(8,128)(2,1)S(1)}, u32[]{:S(2)}, u32[]{:S(2)}) collective-permute-start(bf16[272,256]{1,0:T(8,128)(2,1)S(1)} %get-tuple-element.30), channel_id=1, source_target_pairs={{1,2},{3,4},{5,6},{7,8},{9,10},{11,12},{13,14},{2,1},{4,3},{6,5},{... | collective-permute-start | bytes 417800 | tf_op jit(solution)/shard_map/ppermute | solution.py:458
  4.7 9.2 %collective-permute-start.1 = (bf16[272,256]{1,0:T(8,128)(2,1)S(1)}, bf16[272,256]{1,0:T(8,128)(2,1)S(1)}, u32[]{:S(2)}, u32[]{:S(2)}) collective-permute-start(bf16[272,256]{1,0:T(8,128)(2,1)S(1)} %get-tuple-element.31), channel_id=1, source_target_pairs={{0,1},{2,3},{4,5},{6,7},{8,9},{10,11},{12,13},{14,15},{1,0},{3,2},... | collective-permute-start | bytes 417800 | tf_op jit(solution)/shard_map/ppermute | solution.py:458
  13.9 0.0 copy-done.3
  13.9 0.2 reshape_reshape.3.u1b_ref
  14.1 0.2 reshape.22
  14.3 0.0 copy-done.4
  14.3 0.1 reshape.25
  14.5 0.1 copy.11
  14.6 0.1 copy.12
  14.7 0.1 copy.13.ku_ref
  14.8 0.2 copy.10
  14.9 0.0 copy-done.2
  15.0 0.4 %reshape.24.u2_ref = bf16[1728,64]{1,0:T(8,128)(2,1)S(1)} reshape(bf16[27,4096]{1,0:T(8,128)(2,1)S(1)} %copy-done.2) | data formatting | bytes 442368 | tf_op jit(solution)/shard_map/reshape | solution.py:487
  15.4 2.4 %shard_map.66 = (bf16[2048,256]{1,0:T(8,128)(2,1)S(1)}, bf16[2048,256]{1,0:T(8,128)(2,1)S(1)}, bf16[2304,128]{1,0:T(8,128)(2,1)S(1)}, bf16[2304,128]{1,0:T(8,128...) custom-call(bf16[864,32]{1,0:T(8,128)(2,1)S(1)} %bitcast.10, ...), custom_call_target="tpu_custom_call" | custom-call | flops 1000000000 | bytes 10000000 | tf_op jit(solution)/shard_map/pallas_call | solution.py:436
  17.8 0.0 collective-permute-done.ya_ref
  17.8 0.0 collective-permute-done.1.yb_ref
  17.8 1.6 %shard_map.67 = (bf16[304,256]{1,0:T(8,128)(2,1)S(1)}, bf16[304,256]{1,0:T(8,128)(2,1)S(1)}, bf16[4,96,128]{2,1,0:T(8,128)(2,1)S(1)}, bf16[128,128]{1,0:T(8,128)...) custom-call(s32[1]{0:T(128)} %bitcast.9.flag_ref, ...), custom_call_target="tpu_custom_call" | custom-call | flops 500000000 | bytes 1000000 | tf_op jit(solution)/shard_map/pallas_call | solution.py:436
  19.5 4.2 %collective-permute-start.2 = (bf16[304,256]{1,0:T(8,128)(2,1)S(1)}, bf16[304,256]{1,0:T(8,128)(2,1)S(1)}, u32[]{:S(2)}, u32[]{:S(2)}) collective-permute-start(bf16[304,256]{1,0:T(8,128)(2,1)S(1)} %get-tuple-element.34), channel_id=1, source_target_pairs={{16,32},{48,64},{80,96},{112,128},{144,160},{176,192},{208,224},{2... | collective-permute-start | bytes 466952 | tf_op jit(solution)/shard_map/ppermute | solution.py:458
  23.7 3.3 %collective-permute-start.3 = (bf16[304,256]{1,0:T(8,128)(2,1)S(1)}, bf16[304,256]{1,0:T(8,128)(2,1)S(1)}, u32[]{:S(2)}, u32[]{:S(2)}) collective-permute-start(bf16[304,256]{1,0:T(8,128)(2,1)S(1)} %get-tuple-element.35), channel_id=1, source_target_pairs={{0,16},{32,48},{64,80},{96,112},{128,144},{160,176},{192,208},{224... | collective-permute-start | bytes 466952 | tf_op jit(solution)/shard_map/ppermute | solution.py:458
  27.0 1.8 %shard_map.68 = (bf16[9,2,80,128]{3,2,1,0:T(8,128)(2,1)S(1)}, bf16[4,2,64,256]{3,2,1,0:T(8,128)(2,1)S(1)}) custom-call(bf16[4,96,128]{2,1,0:T(8,128)(2,1)S(1)} %get-tuple-element.36.cot_ref.refs_0_, bf16[128,128]{1,0:T(8,128)(2,1)S(1)} %get-tuple-element.37.marks_ref.refs_1_, bf16[4,8,112,256]{3,2,1,0:T(8,128)(2,1)S(1)} %get-tuple-element.38.p_ref.refs_2_, ...), custom_call_target="tpu_custom_call" | custom-call | flops 20000000000 | bytes 10000000 | tf_op jit(solution)/shard_map/pallas_call | solution.py:436
  28.7 0.0 collective-permute-done.3.msg_ref
  28.7 2.9 %shard_map.69.near_ref = f32[2,256,128]{2,1,0:T(8,128)S(1)} custom-call(bf16[304,256]{1,0:T(8,128)(2,1)S(1)} %collective-permute-done.3.msg_ref, bf16[4,96,128]{2,1,0:T(8,128)(2,1)S(1)} %get-tuple-element.36.cot_ref.refs_0_, bf16[128,128]{1,0:T(8,128)(2,1)S(1)} %get-tuple-element.37.marks_ref.refs_1_, ...), custom_call_target="tpu_custom_call" | custom-call | flops 20000000000 | bytes 10000000 | tf_op jit(solution)/shard_map/pallas_call | solution.py:436
  31.6 0.0 collective-permute-done.2.msg_ref
  31.6 3.6 %shard_map.70 = bf16[32,16,256]{2,1,0:T(8,128)(2,1)} custom-call(bf16[304,256]{1,0:T(8,128)(2,1)S(1)} %collective-permute-done.2.msg_ref, f32[2,256,128]{2,1,0:T(8,128)S(1)} %shard_map.69.near_ref, bf16[4,96,128]{2,1,0:T(8,128)(2,1)S(1)} %get-tuple-element.36.cot_ref.refs_0_, bf16[128,128]{1,0:T(8,128)(2,1)S(1)} %get-tuple-element.37.marks_ref.refs_1_, ...), custom_call_target="tpu_custom_call" | custom-call | flops 10000000000 | bytes 10000000 | tf_op jit(solution)/shard_map/pallas_call | solution.py:436
Async XLA Ops:
  0.0 0.9 %copy-start.1 = (bf16[64,8,64]{2,1,0:T(8,128)(2,1)S(1)}, bf16[64,8,64]{2,1,0:T(8,128)(2,1)}, u32[]{:S(2)}) copy-start(bf16[64,8,64]{2,1,0:T(8,128)(2,1)} %cot_ref.1) | copy-start | bytes 196612
  0.0 1.0 %copy-start = (bf16[32,16,256]{2,1,0:T(8,128)(2,1)S(1)}, bf16[32,16,256]{2,1,0:T(8,128)(2,1)}, u32[]{:S(2)}) copy-start(bf16[32,16,256]{2,1,0:T(8,128)(2,1)} %feat_ref.1) | copy-start | bytes 786436
  1.0 12.9 %copy-start.3 = (bf16[27,1024]{1,0:T(8,128)(2,1)S(1)}, bf16[27,1024]{1,0:T(8,128)(2,1)}, u32[]{:S(2)}) copy-start(bf16[27,1024]{1,0:T(8,128)(2,1)} %param.8) | copy-start | bytes 165892
  1.0 13.3 %copy-start.4 = (bf16[8,2048]{1,0:T(8,128)(2,1)S(1)}, bf16[8,2048]{1,0:T(8,128)(2,1)}, u32[]{:S(2)}) copy-start(bf16[8,2048]{1,0:T(8,128)(2,1)} %param.9) | copy-start | bytes 98308
  1.6 13.4 %copy-start.2 = (bf16[27,4096]{1,0:T(8,128)(2,1)S(1)}, bf16[27,4096]{1,0:T(8,128)(2,1)}, u32[]{:S(2)}) copy-start(bf16[27,4096]{1,0:T(8,128)(2,1)} %param.10) | copy-start | bytes 663556
  1.6 16.2 %collective-permute-start = (bf16[272,256]{1,0:T(8,128)(2,1)S(1)}, bf16[272,256]{1,0:T(8,128)(2,1)S(1)}, u32[]{:S(2)}, u32[]{:S(2)}) collective-permute-start(bf16[272,256]{1,0:T(8,128)(2,1)S(1)} %get-tuple-element.30), channel_id=1, source_target_pairs={{1,2},{3,4},{5,6},{7,8},{9,10},{11,12},{13,14},{2,1},{4,3},{6,5},{... | collective-permute-start | bytes 417800 | tf_op jit(solution)/shard_map/ppermute | solution.py:458
  4.7 13.1 %collective-permute-start.1 = (bf16[272,256]{1,0:T(8,128)(2,1)S(1)}, bf16[272,256]{1,0:T(8,128)(2,1)S(1)}, u32[]{:S(2)}, u32[]{:S(2)}) collective-permute-start(bf16[272,256]{1,0:T(8,128)(2,1)S(1)} %get-tuple-element.31), channel_id=1, source_target_pairs={{0,1},{2,3},{4,5},{6,7},{8,9},{10,11},{12,13},{14,15},{1,0},{3,2},... | collective-permute-start | bytes 417800 | tf_op jit(solution)/shard_map/ppermute | solution.py:458
  19.5 12.2 %collective-permute-start.2 = (bf16[304,256]{1,0:T(8,128)(2,1)S(1)}, bf16[304,256]{1,0:T(8,128)(2,1)S(1)}, u32[]{:S(2)}, u32[]{:S(2)}) collective-permute-start(bf16[304,256]{1,0:T(8,128)(2,1)S(1)} %get-tuple-element.34), channel_id=1, source_target_pairs={{16,32},{48,64},{80,96},{112,128},{144,160},{176,192},{208,224},{2... | collective-permute-start | bytes 466952 | tf_op jit(solution)/shard_map/ppermute | solution.py:458
  23.7 5.0 %collective-permute-start.3 = (bf16[304,256]{1,0:T(8,128)(2,1)S(1)}, bf16[304,256]{1,0:T(8,128)(2,1)S(1)}, u32[]{:S(2)}, u32[]{:S(2)}) collective-permute-start(bf16[304,256]{1,0:T(8,128)(2,1)S(1)} %get-tuple-element.35), channel_id=1, source_target_pairs={{0,16},{32,48},{64,80},{96,112},{128,144},{160,176},{192,208},{224... | collective-permute-start | bytes 466952 | tf_op jit(solution)/shard_map/ppermute | solution.py:458

commit v4 on v3

--- a/solution.py
+++ b/solution.py
@@ -103,7 +103,12 @@
 
 def fine_weights(u_ref, out_ref, u_scr, v_scr, w_scr, backward):
     tile = one_hot(iota((32, 256), 0) == iota((32, 256), 1) % 32)
-    u_scr[...] = dot(u_ref[...], tile).astype(BF16).reshape(27, 32, 256)
+    taps_in = u_ref[...]
+    if not backward:
+        eye = one_hot(iota((32, 32), 0) == iota((32, 32), 1))
+        turned = lax.dot_general(eye, taps_in, NT, preferred_element_type=F32)
+        taps_in = jnp.concatenate([turned[:, 32 * e : 32 * e + 32] for e in range(27)], axis=0).astype(BF16)
+    u_scr[...] = dot(taps_in, tile).astype(BF16).reshape(27, 32, 256)
     lane = iota((32, 256), 1)
     low2 = one_hot((lane // 32) % 2 == 0), one_hot((lane // 32) % 2 == 1)
     low1 = one_hot((lane // 64) % 2 == 0), one_hot((lane // 64) % 2 == 1)
@@ -169,20 +174,24 @@
 
 
 def weight_kernel(
-    u1_ref, u1b_ref, u2_ref, kd_ref, ku_ref,
+    u1_ref, u2_ref, ud_ref,
     w1_ref, w2_ref, w3_ref, w4_ref, wd_ref, wu_ref,
     u_scr, v_scr, w_scr, uc_scr,
 ):
     fine_weights(u1_ref, w1_ref, u_scr, v_scr, w_scr, False)
-    fine_weights(u1b_ref, w2_ref, u_scr, v_scr, w_scr, True)
+    fine_weights(u1_ref, w2_ref, u_scr, v_scr, w_scr, True)
     coarse_weights(u2_ref, w3_ref, uc_scr, False)
     coarse_weights(u2_ref, w4_ref, uc_scr, True)
+    lane = iota((32, 256), 1)
+    up = sum(
+        dot(ud_ref[pl.ds(64 * a, 64), :], one_hot(iota((32, 256), 0) + 32 * a == lane)) for a in range(8)
+    ).astype(BF16)
     for b in range(2):
         place = one_hot(iota((64, 128), 0) + 64 * b == iota((64, 128), 1))
-        wd_ref[pl.ds(256 * b, 256), :] = dot(kd_ref[...], place).astype(BF16)
-        zero = jnp.zeros((64, 256), BF16)
-        wu_ref[b, pl.ds(64 * b, 64), :] = ku_ref[...]
-        wu_ref[b, pl.ds(64 * (1 - b), 64), :] = zero
+        turned = lax.dot_general(up, place, TN, preferred_element_type=F32)
+        wd_ref[pl.ds(256 * b, 256), :] = turned.astype(BF16)
+        wu_ref[b, pl.ds(64 * b, 64), :] = up
+        wu_ref[b, pl.ds(64 * (1 - b), 64), :] = jnp.zeros((64, 256), BF16)
 
 
 def silu_parts(v):
@@ -469,11 +478,9 @@
         2 * 10**9, 10**6, flag, features, cotangent, q, parity,
     )
     y_a, y_b = swaps(y_first, y_second, "gy")
-    fine = kernel_fine.reshape(27, C1, C1)
-    down = kernel_down.reshape(8, C2, C1)
     w1, w2, w3, w4, wd, wu = call(
         weight_kernel,
-        [VMEM] * 5,
+        [VMEM] * 3,
         [shape(2048, 256), shape(2048, 256), shape(2304, 128), shape(2304, 128), shape(512, 128), shape(2, 128, 256)],
         [
             pltpu.VMEM((27, 32, 256), BF16),
@@ -482,11 +489,9 @@
             pltpu.VMEM((27, 64, 128), BF16),
         ],
         10**9, 10**7,
-        fine.transpose(0, 2, 1).reshape(27 * C1, C1),
-        fine.reshape(27 * C1, C1),
+        kernel_fine.reshape(27 * C1, C1),
         kernel_coarse.reshape(27 * C2, C2),
-        down.transpose(0, 2, 1).reshape(8 * C1, C2),
-        down.transpose(1, 0, 2).reshape(C2, 8 * C1),
+        kernel_down.reshape(8 * C2, C1),
     )
     x_first, x_second, cot, marks, pe, dve, de = call(
         edge_kernel,

time: 35.5 us -> 35.2 us (level)
  local copies, waits for them, and re-layouts: 1.66 us -> 1.01 us
  Pallas kernels: 12.9 us -> 13.5 us
    pallas_call x7, Pallas kernels: 12.9 us -> 13.5 us  [call(): pl.pallas_call(kernel, out_shape=outs, in_specs=specs, out_specs=jax.tree...]
  transfers between devices with their start and end apart: 4 -> 4, of which waited for: 0 -> 0; matrix products, arithmetic and copies ran while one was open for 4% -> 2% of each run, Pallas kernels for 20% -> 22%
where the time goes in v4:
time: 35.2 us; the launch traced here: 35 us
  starting transfers between devices  19.6 us (56%)
  Pallas kernels  13.5 us (38%)
  local copies, waits for them, and re-layouts  1.01 us (3%)
  between operations  0.85 us (2%)
    pallas_call x7, Pallas kernels, call(): pl.pallas_call(kernel, out_shape=outs, in_specs=specs, out_specs=jax.tree...  13.5 us
    ppermute x2, starting transfers between devices, swaps(): lax.ppermute(second, axis, both_ways(0))  12.4 us
    ppermute x2, starting transfers between devices, swaps(): lax.ppermute(first, axis, both_ways(1))  7.2 us
  transfers between devices with their start and end apart: 4, of which 0 were waited for; matrix products, arithmetic and copies ran while one was open for 2% of the time, Pallas kernels for 22%

profile of v4, /device:TPU:55, one launch (start us, length us, event | category | flops | bytes accessed | tf_op | source)
XLA Modules:
  0.0 35.0 jit_solution(11298625072953751571)
XLA Ops:
  0.0 0.0 copy-start.1
  0.0 0.0 copy-start
  0.0 0.1 shard_map.64
  0.8 0.1 copy-done.1
  0.9 0.1 copy-done
  1.0 0.0 copy-start.4
  1.0 0.0 copy-start.3
  1.0 0.0 copy-start.2
  1.0 0.6 %shard_map.65 = (bf16[8,64,256]{2,1,0:T(8,128)(2,1)S(1)}, bf16[4,64,128]{2,1,0:T(8,128)(2,1)S(1)}, bf16[272,256]{1,0:T(8,128)(2,1)S(1)}, bf16[272,256]{1,0:T(8,128)(2,1)S(1)}) custom-call(s32[1]{0:T(128)} %bitcast.1.flag_ref, bf16[32,16,256]{2,1,0:T(8,128)(2,1)S(1)} %copy-done, bf16[64,8,64]{2,1,0:T(8,128)(2,1)S(1)} %copy-done.1, ...), custom_call_target="tpu_custom_call" | custom-call | flops 2000000000 | bytes 1000000 | tf_op jit(solution)/shard_map/pallas_call | solution.py:445
  1.6 3.0 %collective-permute-start = (bf16[272,256]{1,0:T(8,128)(2,1)S(1)}, bf16[272,256]{1,0:T(8,128)(2,1)S(1)}, u32[]{:S(2)}, u32[]{:S(2)}) collective-permute-start(bf16[272,256]{1,0:T(8,128)(2,1)S(1)} %get-tuple-element.30), channel_id=1, source_target_pairs={{1,2},{3,4},{5,6},{7,8},{9,10},{11,12},{13,14},{2,1},{4,3},{6,5},{... | collective-permute-start | bytes 417800 | tf_op jit(solution)/shard_map/ppermute | solution.py:467
  4.6 9.2 %collective-permute-start.1 = (bf16[272,256]{1,0:T(8,128)(2,1)S(1)}, bf16[272,256]{1,0:T(8,128)(2,1)S(1)}, u32[]{:S(2)}, u32[]{:S(2)}) collective-permute-start(bf16[272,256]{1,0:T(8,128)(2,1)S(1)} %get-tuple-element.31), channel_id=1, source_target_pairs={{0,1},{2,3},{4,5},{6,7},{8,9},{10,11},{12,13},{14,15},{1,0},{3,2},... | collective-permute-start | bytes 417800 | tf_op jit(solution)/shard_map/ppermute | solution.py:467
  13.8 0.0 copy-done.4
  13.8 0.1 reshape.15.ud_ref
  13.9 0.0 copy-done.3
  13.9 0.2 reshape.13.u1_ref
  14.1 0.0 copy-done.2
  14.1 0.4 %reshape.14.u2_ref = bf16[1728,64]{1,0:T(8,128)(2,1)S(1)} reshape(bf16[27,4096]{1,0:T(8,128)(2,1)S(1)} %copy-done.2) | data formatting | bytes 442368 | tf_op jit(solution)/shard_map/reshape | solution.py:493
  14.6 3.0 %shard_map.66 = (bf16[2048,256]{1,0:T(8,128)(2,1)S(1)}, bf16[2048,256]{1,0:T(8,128)(2,1)S(1)}, bf16[2304,128]{1,0:T(8,128)(2,1)S(1)}, bf16[2304,128]{1,0:T(8,128...) custom-call(bf16[864,32]{1,0:T(8,128)(2,1)S(1)} %reshape.13.u1_ref, ...), custom_call_target="tpu_custom_call" | custom-call | flops 1000000000 | bytes 10000000 | tf_op jit(solution)/shard_map/pallas_call | solution.py:445
  17.6 0.0 collective-permute-done.ya_ref
  17.6 0.0 collective-permute-done.1.yb_ref
  17.6 1.6 %shard_map.67 = (bf16[304,256]{1,0:T(8,128)(2,1)S(1)}, bf16[304,256]{1,0:T(8,128)(2,1)S(1)}, bf16[4,96,128]{2,1,0:T(8,128)(2,1)S(1)}, bf16[128,128]{1,0:T(8,128)...) custom-call(s32[1]{0:T(128)} %bitcast.2.flag_ref, ...), custom_call_target="tpu_custom_call" | custom-call | flops 500000000 | bytes 1000000 | tf_op jit(solution)/shard_map/pallas_call | solution.py:445
  19.2 4.2 %collective-permute-start.2 = (bf16[304,256]{1,0:T(8,128)(2,1)S(1)}, bf16[304,256]{1,0:T(8,128)(2,1)S(1)}, u32[]{:S(2)}, u32[]{:S(2)}) collective-permute-start(bf16[304,256]{1,0:T(8,128)(2,1)S(1)} %get-tuple-element.34), channel_id=1, source_target_pairs={{16,32},{48,64},{80,96},{112,128},{144,160},{176,192},{208,224},{2... | collective-permute-start | bytes 466952 | tf_op jit(solution)/shard_map/ppermute | solution.py:467
  23.5 3.3 %collective-permute-start.3 = (bf16[304,256]{1,0:T(8,128)(2,1)S(1)}, bf16[304,256]{1,0:T(8,128)(2,1)S(1)}, u32[]{:S(2)}, u32[]{:S(2)}) collective-permute-start(bf16[304,256]{1,0:T(8,128)(2,1)S(1)} %get-tuple-element.35), channel_id=1, source_target_pairs={{0,16},{32,48},{64,80},{96,112},{128,144},{160,176},{192,208},{224... | collective-permute-start | bytes 466952 | tf_op jit(solution)/shard_map/ppermute | solution.py:467
  26.7 1.8 %shard_map.68 = (bf16[9,2,80,128]{3,2,1,0:T(8,128)(2,1)S(1)}, bf16[4,2,64,256]{3,2,1,0:T(8,128)(2,1)S(1)}) custom-call(bf16[4,96,128]{2,1,0:T(8,128)(2,1)S(1)} %get-tuple-element.36.cot_ref.refs_0_, bf16[128,128]{1,0:T(8,128)(2,1)S(1)} %get-tuple-element.37.marks_ref.refs_1_, bf16[4,8,112,256]{3,2,1,0:T(8,128)(2,1)S(1)} %get-tuple-element.38.p_ref.refs_2_, ...), custom_call_target="tpu_custom_call" | custom-call | flops 20000000000 | bytes 10000000 | tf_op jit(solution)/shard_map/pallas_call | solution.py:445
  28.5 0.0 collective-permute-done.3.msg_ref
  28.5 2.9 %shard_map.69.near_ref = f32[2,256,128]{2,1,0:T(8,128)S(1)} custom-call(bf16[304,256]{1,0:T(8,128)(2,1)S(1)} %collective-permute-done.3.msg_ref, bf16[4,96,128]{2,1,0:T(8,128)(2,1)S(1)} %get-tuple-element.36.cot_ref.refs_0_, bf16[128,128]{1,0:T(8,128)(2,1)S(1)} %get-tuple-element.37.marks_ref.refs_1_, ...), custom_call_target="tpu_custom_call" | custom-call | flops 20000000000 | bytes 10000000 | tf_op jit(solution)/shard_map/pallas_call | solution.py:445
  31.4 0.0 collective-permute-done.2.msg_ref
  31.4 3.6 %shard_map.70 = bf16[32,16,256]{2,1,0:T(8,128)(2,1)} custom-call(bf16[304,256]{1,0:T(8,128)(2,1)S(1)} %collective-permute-done.2.msg_ref, f32[2,256,128]{2,1,0:T(8,128)S(1)} %shard_map.69.near_ref, bf16[4,96,128]{2,1,0:T(8,128)(2,1)S(1)} %get-tuple-element.36.cot_ref.refs_0_, bf16[128,128]{1,0:T(8,128)(2,1)S(1)} %get-tuple-element.37.marks_ref.refs_1_, ...), custom_call_target="tpu_custom_call" | custom-call | flops 10000000000 | bytes 10000000 | tf_op jit(solution)/shard_map/pallas_call | solution.py:445
Async XLA Ops:
  0.0 0.9 %copy-start.1 = (bf16[64,8,64]{2,1,0:T(8,128)(2,1)S(1)}, bf16[64,8,64]{2,1,0:T(8,128)(2,1)}, u32[]{:S(2)}) copy-start(bf16[64,8,64]{2,1,0:T(8,128)(2,1)} %cot_ref.1) | copy-start | bytes 196612
  0.0 1.0 %copy-start = (bf16[32,16,256]{2,1,0:T(8,128)(2,1)S(1)}, bf16[32,16,256]{2,1,0:T(8,128)(2,1)}, u32[]{:S(2)}) copy-start(bf16[32,16,256]{2,1,0:T(8,128)(2,1)} %feat_ref.1) | copy-start | bytes 786436
  1.0 12.7 %copy-start.4 = (bf16[8,2048]{1,0:T(8,128)(2,1)S(1)}, bf16[8,2048]{1,0:T(8,128)(2,1)}, u32[]{:S(2)}) copy-start(bf16[8,2048]{1,0:T(8,128)(2,1)} %param.9) | copy-start | bytes 98308
  1.0 12.9 %copy-start.3 = (bf16[27,1024]{1,0:T(8,128)(2,1)S(1)}, bf16[27,1024]{1,0:T(8,128)(2,1)}, u32[]{:S(2)}) copy-start(bf16[27,1024]{1,0:T(8,128)(2,1)} %param.8) | copy-start | bytes 165892
  1.0 13.1 %copy-start.2 = (bf16[27,4096]{1,0:T(8,128)(2,1)S(1)}, bf16[27,4096]{1,0:T(8,128)(2,1)}, u32[]{:S(2)}) copy-start(bf16[27,4096]{1,0:T(8,128)(2,1)} %param.10) | copy-start | bytes 663556
  1.6 16.0 %collective-permute-start = (bf16[272,256]{1,0:T(8,128)(2,1)S(1)}, bf16[272,256]{1,0:T(8,128)(2,1)S(1)}, u32[]{:S(2)}, u32[]{:S(2)}) collective-permute-start(bf16[272,256]{1,0:T(8,128)(2,1)S(1)} %get-tuple-element.30), channel_id=1, source_target_pairs={{1,2},{3,4},{5,6},{7,8},{9,10},{11,12},{13,14},{2,1},{4,3},{6,5},{... | collective-permute-start | bytes 417800 | tf_op jit(solution)/shard_map/ppermute | solution.py:467
  4.6 13.0 %collective-permute-start.1 = (bf16[272,256]{1,0:T(8,128)(2,1)S(1)}, bf16[272,256]{1,0:T(8,128)(2,1)S(1)}, u32[]{:S(2)}, u32[]{:S(2)}) collective-permute-start(bf16[272,256]{1,0:T(8,128)(2,1)S(1)} %get-tuple-element.31), channel_id=1, source_target_pairs={{0,1},{2,3},{4,5},{6,7},{8,9},{10,11},{12,13},{14,15},{1,0},{3,2},... | collective-permute-start | bytes 417800 | tf_op jit(solution)/shard_map/ppermute | solution.py:467
  19.2 12.2 %collective-permute-start.2 = (bf16[304,256]{1,0:T(8,128)(2,1)S(1)}, bf16[304,256]{1,0:T(8,128)(2,1)S(1)}, u32[]{:S(2)}, u32[]{:S(2)}) collective-permute-start(bf16[304,256]{1,0:T(8,128)(2,1)S(1)} %get-tuple-element.34), channel_id=1, source_target_pairs={{16,32},{48,64},{80,96},{112,128},{144,160},{176,192},{208,224},{2... | collective-permute-start | bytes 466952 | tf_op jit(solution)/shard_map/ppermute | solution.py:467
  23.5 5.0 %collective-permute-start.3 = (bf16[304,256]{1,0:T(8,128)(2,1)S(1)}, bf16[304,256]{1,0:T(8,128)(2,1)S(1)}, u32[]{:S(2)}, u32[]{:S(2)}) collective-permute-start(bf16[304,256]{1,0:T(8,128)(2,1)S(1)} %get-tuple-element.35), channel_id=1, source_target_pairs={{0,16},{32,48},{64,80},{96,112},{128,144},{160,176},{192,208},{224... | collective-permute-start | bytes 466952 | tf_op jit(solution)/shard_map/ppermute | solution.py:467

commit v5 on v4

--- a/solution.py
+++ b/solution.py
@@ -200,18 +200,23 @@
     return vs, s + vs * (1.0 - s)
 
 
+def keep(shape, cond):
+    return jnp.where(cond(iota(shape, 1), iota(shape, 2)), 1.0, 0.0)
+
+
 def shift_z(cells, up):
-    z = iota(cells.shape, 1)
+    shape = (1, *cells.shape[1:])
     if up:
-        return jnp.where(z < 7, pltpu.roll(cells, 7, 1), 0.0)
-    return jnp.where(z > 0, pltpu.roll(cells, 1, 1), 0.0)
+        return pltpu.roll(cells, 7, 1) * keep(shape, lambda z, lane: z < 7)
+    return pltpu.roll(cells, 1, 1) * keep(shape, lambda z, lane: z > 0)
 
 
 def mixed(cells, store):
     n = cells.shape[0]
     rows = (n - 2) * 8
-    lane = iota(cells.shape, 2)
-    zmix = jnp.where((lane // 32) % 2 == 0, shift_z(cells, True), shift_z(cells, False))
+    low = keep((1, 8, 256), lambda z, lane: ((lane // 32) % 2 == 0) & (z < 7))
+    high = keep((1, 8, 256), lambda z, lane: ((lane // 32) % 2 == 1) & (z > 0))
+    zmix = pltpu.roll(cells, 7, 1) * low + pltpu.roll(cells, 1, 1) * high
     low1 = (iota((n - 2, 8, 256), 2) // 64) % 2 == 0
     for mz, form in enumerate((cells, zmix)):
         store(mz, form[1 : n - 1].reshape(rows, 256).astype(BF16))
@@ -352,7 +357,7 @@
 
 
 def side_steps(
-    side, msg_ref, cot_ref, marks_ref, pe_ref, dve_ref, de_ref, gm_ref, qm_ref, q_ref, parity_ref,
+    side, msg_ref, cot_ref, marks_ref, pe_ref, dve_ref, de_ref, gm_ref, qm_ref, q_ref,
     w1_ref, w2_ref, w3_ref, w4_ref, wd_ref, wu_ref,
     store_out, scratch,
 ):
@@ -394,18 +399,23 @@
     grad = dot(lhs, w4_ref[...]).astype(BF16)
     for k in range(2):
         fine_gradient(grad[80 * k : 80 * k + 80], lambda b: dv_scr[2 * k + b], wu_ref, q_scr, 2 * side + 2 * k)
-    lhs = jnp.concatenate([conv_lhs(*((q_scr, k + n) for n in range(3))) for k in range(4)], axis=0)
-    grad = dot(lhs, w2_ref[...]).astype(BF16)
-    parity = parity_ref[...].astype(F32)
-    for k in range(4):
-        spread = lax.dot_general(grad[64 * k : 64 * k + 64], q_ref[...], TN, preferred_element_type=F32) * parity
-        for b in range(2):
-            rows = sum(spread[128 * b + 32 * i : 128 * b + 32 * i + 32] for i in range(4))
-            store_out(2 * k + b, rows)
+    lane = iota((32, 256), 1)
+    low_y_cell, low_z_cell = (lane // 16) % 2 == 0, lane % 2 == 0
+    for h in range(2):
+        lhs = jnp.concatenate(
+            [conv_lhs(*((q_scr, 2 * h + k + n) for n in range(3))) for k in range(2)], axis=0
+        )
+        grad = dot(lhs, w2_ref[...]).astype(BF16)
+        for k in range(2):
+            spread = lax.dot_general(grad[64 * k : 64 * k + 64], q_ref[...], TN, preferred_element_type=F32)
+            for b in range(2):
+                rows = [spread[128 * b + 32 * i : 128 * b + 32 * i + 32] for i in range(4)]
+                pairs = [jnp.where(low_z_cell, rows[i], rows[i + 1]) for i in (0, 2)]
+                store_out(4 * h + 2 * k + b, jnp.where(low_y_cell, *pairs))
 
 
 def near_kernel(msg_ref, *refs):
-    inputs, out_ref, scratch = refs[:15], refs[15], refs[16:]
+    inputs, out_ref, scratch = refs[:14], refs[14], refs[15:]
 
     def store_out(x, rows):
         for h in range(2):
@@ -415,7 +425,7 @@
 
 
 def far_kernel(msg_ref, near_ref, *refs):
-    inputs, out_ref, scratch, o_scr = refs[:15], refs[15], refs[16:-1], refs[-1]
+    inputs, out_ref, scratch, o_scr = refs[:14], refs[14], refs[15:-1], refs[-1]
     side = is_odd("gx")
     o_scr[1 - side] = near_ref[...]
 
@@ -512,17 +522,17 @@
         2 * 10**10, 10**7,
         cot, marks, pe, de, w1, w3, w4, wd, wu,
     )
-    shared = (cot, marks, pe, dve, de, gm, qm, q, parity, w1, w2, w3, w4, wd, wu)
+    shared = (cot, marks, pe, dve, de, gm, qm, q, w1, w2, w3, w4, wd, wu)
     near = call(
         near_kernel,
-        [VMEM] * 16,
+        [VMEM] * 15,
         shape(2, 256, 128, dtype=F32),
         SIDE_SCRATCH,
         2 * 10**10, 10**7, x_b, *shared,
     )
     return call(
         far_kernel,
-        [VMEM] * 17,
+        [VMEM] * 16,
         shape(32, 16, 256),
         SIDE_SCRATCH + [pltpu.VMEM((2, 2, 256, 128), F32)],
         10**10, 10**7, x_a, near, *shared,

time: 35.2 us -> 35.9 us (1.020)
  Pallas kernels: 13.5 us -> 14.1 us
    pallas_call x7, Pallas kernels: 13.5 us -> 14.1 us  [call(): pl.pallas_call(kernel, out_shape=outs, in_specs=specs, out_specs=jax.tree...]
where the time goes in v5:
time: 35.9 us; the launch traced here: 35.7 us
  starting transfers between devices  19.6 us (55%)
  Pallas kernels  14.1 us (39%)
  local copies, waits for them, and re-layouts  1.01 us (3%)
  between operations  0.85 us (2%)
    pallas_call x7, Pallas kernels, call(): pl.pallas_call(kernel, out_shape=outs, in_specs=specs, out_specs=jax.tree...  14.1 us
    ppermute x2, starting transfers between devices, swaps(): lax.ppermute(second, axis, both_ways(0))  12.4 us
    ppermute x2, starting transfers between devices, swaps(): lax.ppermute(first, axis, both_ways(1))  7.21 us
  transfers between devices with their start and end apart: 4, of which 0 were waited for; matrix products, arithmetic and copies ran while one was open for 2% of the time, Pallas kernels for 22%

profile of v5, /device:TPU:55, one launch (start us, length us, event | category | flops | bytes accessed | tf_op | source)
XLA Modules:
  0.0 35.7 jit_solution(13433614035226370879)
XLA Ops:
  0.0 0.0 copy-start.1
  0.0 0.0 copy-start
  0.0 0.1 shard_map.64
  0.8 0.1 copy-done.1
  0.9 0.1 copy-done
  1.0 0.0 copy-start.4
  1.0 0.0 copy-start.3
  1.0 0.0 copy-start.2
  1.0 0.6 %shard_map.65 = (bf16[8,64,256]{2,1,0:T(8,128)(2,1)S(1)}, bf16[4,64,128]{2,1,0:T(8,128)(2,1)S(1)}, bf16[272,256]{1,0:T(8,128)(2,1)S(1)}, bf16[272,256]{1,0:T(8,128)(2,1)S(1)}) custom-call(s32[1]{0:T(128)} %bitcast.1.flag_ref, bf16[32,16,256]{2,1,0:T(8,128)(2,1)S(1)} %copy-done, bf16[64,8,64]{2,1,0:T(8,128)(2,1)S(1)} %copy-done.1, ...), custom_call_target="tpu_custom_call" | custom-call | flops 2000000000 | bytes 1000000 | tf_op jit(solution)/shard_map/pallas_call | solution.py:455
  1.6 3.0 %collective-permute-start = (bf16[272,256]{1,0:T(8,128)(2,1)S(1)}, bf16[272,256]{1,0:T(8,128)(2,1)S(1)}, u32[]{:S(2)}, u32[]{:S(2)}) collective-permute-start(bf16[272,256]{1,0:T(8,128)(2,1)S(1)} %get-tuple-element.30), channel_id=1, source_target_pairs={{1,2},{3,4},{5,6},{7,8},{9,10},{11,12},{13,14},{2,1},{4,3},{6,5},{... | collective-permute-start | bytes 417800 | tf_op jit(solution)/shard_map/ppermute | solution.py:477
  4.6 9.2 %collective-permute-start.1 = (bf16[272,256]{1,0:T(8,128)(2,1)S(1)}, bf16[272,256]{1,0:T(8,128)(2,1)S(1)}, u32[]{:S(2)}, u32[]{:S(2)}) collective-permute-start(bf16[272,256]{1,0:T(8,128)(2,1)S(1)} %get-tuple-element.31), channel_id=1, source_target_pairs={{0,1},{2,3},{4,5},{6,7},{8,9},{10,11},{12,13},{14,15},{1,0},{3,2},... | collective-permute-start | bytes 417800 | tf_op jit(solution)/shard_map/ppermute | solution.py:477
  13.8 0.0 copy-done.4
  13.8 0.1 reshape.15.ud_ref
  13.9 0.0 copy-done.3
  13.9 0.2 reshape.13.u1_ref
  14.1 0.0 copy-done.2
  14.1 0.4 %reshape.14.u2_ref = bf16[1728,64]{1,0:T(8,128)(2,1)S(1)} reshape(bf16[27,4096]{1,0:T(8,128)(2,1)S(1)} %copy-done.2) | data formatting | bytes 442368 | tf_op jit(solution)/shard_map/reshape | solution.py:503
  14.6 3.0 %shard_map.66 = (bf16[2048,256]{1,0:T(8,128)(2,1)S(1)}, bf16[2048,256]{1,0:T(8,128)(2,1)S(1)}, bf16[2304,128]{1,0:T(8,128)(2,1)S(1)}, bf16[2304,128]{1,0:T(8,128...) custom-call(bf16[864,32]{1,0:T(8,128)(2,1)S(1)} %reshape.13.u1_ref, ...), custom_call_target="tpu_custom_call" | custom-call | flops 1000000000 | bytes 10000000 | tf_op jit(solution)/shard_map/pallas_call | solution.py:455
  17.6 0.0 collective-permute-done.ya_ref
  17.6 0.0 collective-permute-done.1.yb_ref
  17.6 1.6 %shard_map.67 = (bf16[304,256]{1,0:T(8,128)(2,1)S(1)}, bf16[304,256]{1,0:T(8,128)(2,1)S(1)}, bf16[4,96,128]{2,1,0:T(8,128)(2,1)S(1)}, bf16[128,128]{1,0:T(8,128)...) custom-call(s32[1]{0:T(128)} %bitcast.2.flag_ref, ...), custom_call_target="tpu_custom_call" | custom-call | flops 500000000 | bytes 1000000 | tf_op jit(solution)/shard_map/pallas_call | solution.py:455
  19.2 4.2 %collective-permute-start.2 = (bf16[304,256]{1,0:T(8,128)(2,1)S(1)}, bf16[304,256]{1,0:T(8,128)(2,1)S(1)}, u32[]{:S(2)}, u32[]{:S(2)}) collective-permute-start(bf16[304,256]{1,0:T(8,128)(2,1)S(1)} %get-tuple-element.34), channel_id=1, source_target_pairs={{16,32},{48,64},{80,96},{112,128},{144,160},{176,192},{208,224},{2... | collective-permute-start | bytes 466952 | tf_op jit(solution)/shard_map/ppermute | solution.py:477
  23.5 3.3 %collective-permute-start.3 = (bf16[304,256]{1,0:T(8,128)(2,1)S(1)}, bf16[304,256]{1,0:T(8,128)(2,1)S(1)}, u32[]{:S(2)}, u32[]{:S(2)}) collective-permute-start(bf16[304,256]{1,0:T(8,128)(2,1)S(1)} %get-tuple-element.35), channel_id=1, source_target_pairs={{0,16},{32,48},{64,80},{96,112},{128,144},{160,176},{192,208},{224... | collective-permute-start | bytes 466952 | tf_op jit(solution)/shard_map/ppermute | solution.py:477
  26.7 1.8 %shard_map.68 = (bf16[9,2,80,128]{3,2,1,0:T(8,128)(2,1)S(1)}, bf16[4,2,64,256]{3,2,1,0:T(8,128)(2,1)S(1)}) custom-call(bf16[4,96,128]{2,1,0:T(8,128)(2,1)S(1)} %get-tuple-element.36.cot_ref.refs_0_, bf16[128,128]{1,0:T(8,128)(2,1)S(1)} %get-tuple-element.37.marks_ref.refs_1_, bf16[4,8,112,256]{3,2,1,0:T(8,128)(2,1)S(1)} %get-tuple-element.38.p_ref.refs_2_, ...), custom_call_target="tpu_custom_call" | custom-call | flops 20000000000 | bytes 10000000 | tf_op jit(solution)/shard_map/pallas_call | solution.py:455
  28.5 0.0 collective-permute-done.3.msg_ref
  28.5 3.2 %shard_map.69.near_ref = f32[2,256,128]{2,1,0:T(8,128)S(1)} custom-call(bf16[304,256]{1,0:T(8,128)(2,1)S(1)} %collective-permute-done.3.msg_ref, bf16[4,96,128]{2,1,0:T(8,128)(2,1)S(1)} %get-tuple-element.36.cot_ref.refs_0_, bf16[128,128]{1,0:T(8,128)(2,1)S(1)} %get-tuple-element.37.marks_ref.refs_1_, ...), custom_call_target="tpu_custom_call" | custom-call | flops 20000000000 | bytes 10000000 | tf_op jit(solution)/shard_map/pallas_call | solution.py:455
  31.7 0.0 collective-permute-done.2.msg_ref
  31.7 3.9 %shard_map.70 = bf16[32,16,256]{2,1,0:T(8,128)(2,1)} custom-call(bf16[304,256]{1,0:T(8,128)(2,1)S(1)} %collective-permute-done.2.msg_ref, f32[2,256,128]{2,1,0:T(8,128)S(1)} %shard_map.69.near_ref, bf16[4,96,128]{2,1,0:T(8,128)(2,1)S(1)} %get-tuple-element.36.cot_ref.refs_0_, bf16[128,128]{1,0:T(8,128)(2,1)S(1)} %get-tuple-element.37.marks_ref.refs_1_, ...), custom_call_target="tpu_custom_call" | custom-call | flops 10000000000 | bytes 10000000 | tf_op jit(solution)/shard_map/pallas_call | solution.py:455
Async XLA Ops:
  0.0 0.9 %copy-start.1 = (bf16[64,8,64]{2,1,0:T(8,128)(2,1)S(1)}, bf16[64,8,64]{2,1,0:T(8,128)(2,1)}, u32[]{:S(2)}) copy-start(bf16[64,8,64]{2,1,0:T(8,128)(2,1)} %cot_ref.1) | copy-start | bytes 196612
  0.0 1.0 %copy-start = (bf16[32,16,256]{2,1,0:T(8,128)(2,1)S(1)}, bf16[32,16,256]{2,1,0:T(8,128)(2,1)}, u32[]{:S(2)}) copy-start(bf16[32,16,256]{2,1,0:T(8,128)(2,1)} %feat_ref.1) | copy-start | bytes 786436
  1.0 12.7 %copy-start.4 = (bf16[8,2048]{1,0:T(8,128)(2,1)S(1)}, bf16[8,2048]{1,0:T(8,128)(2,1)}, u32[]{:S(2)}) copy-start(bf16[8,2048]{1,0:T(8,128)(2,1)} %param.9) | copy-start | bytes 98308
  1.0 12.9 %copy-start.3 = (bf16[27,1024]{1,0:T(8,128)(2,1)S(1)}, bf16[27,1024]{1,0:T(8,128)(2,1)}, u32[]{:S(2)}) copy-start(bf16[27,1024]{1,0:T(8,128)(2,1)} %param.8) | copy-start | bytes 165892
  1.0 13.1 %copy-start.2 = (bf16[27,4096]{1,0:T(8,128)(2,1)S(1)}, bf16[27,4096]{1,0:T(8,128)(2,1)}, u32[]{:S(2)}) copy-start(bf16[27,4096]{1,0:T(8,128)(2,1)} %param.10) | copy-start | bytes 663556
  1.6 16.0 %collective-permute-start = (bf16[272,256]{1,0:T(8,128)(2,1)S(1)}, bf16[272,256]{1,0:T(8,128)(2,1)S(1)}, u32[]{:S(2)}, u32[]{:S(2)}) collective-permute-start(bf16[272,256]{1,0:T(8,128)(2,1)S(1)} %get-tuple-element.30), channel_id=1, source_target_pairs={{1,2},{3,4},{5,6},{7,8},{9,10},{11,12},{13,14},{2,1},{4,3},{6,5},{... | collective-permute-start | bytes 417800 | tf_op jit(solution)/shard_map/ppermute | solution.py:477
  4.6 13.0 %collective-permute-start.1 = (bf16[272,256]{1,0:T(8,128)(2,1)S(1)}, bf16[272,256]{1,0:T(8,128)(2,1)S(1)}, u32[]{:S(2)}, u32[]{:S(2)}) collective-permute-start(bf16[272,256]{1,0:T(8,128)(2,1)S(1)} %get-tuple-element.31), channel_id=1, source_target_pairs={{0,1},{2,3},{4,5},{6,7},{8,9},{10,11},{12,13},{14,15},{1,0},{3,2},... | collective-permute-start | bytes 417800 | tf_op jit(solution)/shard_map/ppermute | solution.py:477
  19.2 12.5 %collective-permute-start.2 = (bf16[304,256]{1,0:T(8,128)(2,1)S(1)}, bf16[304,256]{1,0:T(8,128)(2,1)S(1)}, u32[]{:S(2)}, u32[]{:S(2)}) collective-permute-start(bf16[304,256]{1,0:T(8,128)(2,1)S(1)} %get-tuple-element.34), channel_id=1, source_target_pairs={{16,32},{48,64},{80,96},{112,128},{144,160},{176,192},{208,224},{2... | collective-permute-start | bytes 466952 | tf_op jit(solution)/shard_map/ppermute | solution.py:477
  23.5 5.1 %collective-permute-start.3 = (bf16[304,256]{1,0:T(8,128)(2,1)S(1)}, bf16[304,256]{1,0:T(8,128)(2,1)S(1)}, u32[]{:S(2)}, u32[]{:S(2)}) collective-permute-start(bf16[304,256]{1,0:T(8,128)(2,1)S(1)} %get-tuple-element.35), channel_id=1, source_target_pairs={{0,16},{32,48},{64,80},{96,112},{128,144},{160,176},{192,208},{224... | collective-permute-start | bytes 466952 | tf_op jit(solution)/shard_map/ppermute | solution.py:477

commit v6 on v4

--- a/solution.py
+++ b/solution.py
@@ -352,7 +352,7 @@
 
 
 def side_steps(
-    side, msg_ref, cot_ref, marks_ref, pe_ref, dve_ref, de_ref, gm_ref, qm_ref, q_ref, parity_ref,
+    side, msg_ref, cot_ref, marks_ref, pe_ref, dve_ref, de_ref, gm_ref, qm_ref, q_ref,
     w1_ref, w2_ref, w3_ref, w4_ref, wd_ref, wu_ref,
     store_out, scratch,
 ):
@@ -396,16 +396,18 @@
         fine_gradient(grad[80 * k : 80 * k + 80], lambda b: dv_scr[2 * k + b], wu_ref, q_scr, 2 * side + 2 * k)
     lhs = jnp.concatenate([conv_lhs(*((q_scr, k + n) for n in range(3))) for k in range(4)], axis=0)
     grad = dot(lhs, w2_ref[...]).astype(BF16)
-    parity = parity_ref[...].astype(F32)
+    lane = iota((32, 256), 1)
+    low_y_cell, low_z_cell = (lane // 16) % 2 == 0, lane % 2 == 0
     for k in range(4):
-        spread = lax.dot_general(grad[64 * k : 64 * k + 64], q_ref[...], TN, preferred_element_type=F32) * parity
+        spread = lax.dot_general(grad[64 * k : 64 * k + 64], q_ref[...], TN, preferred_element_type=F32)
         for b in range(2):
-            rows = sum(spread[128 * b + 32 * i : 128 * b + 32 * i + 32] for i in range(4))
-            store_out(2 * k + b, rows)
+            rows = [spread[128 * b + 32 * i : 128 * b + 32 * i + 32] for i in range(4)]
+            pairs = [jnp.where(low_z_cell, rows[i], rows[i + 1]) for i in (0, 2)]
+            store_out(2 * k + b, jnp.where(low_y_cell, *pairs))
 
 
 def near_kernel(msg_ref, *refs):
-    inputs, out_ref, scratch = refs[:15], refs[15], refs[16:]
+    inputs, out_ref, scratch = refs[:14], refs[14], refs[15:]
 
     def store_out(x, rows):
         for h in range(2):
@@ -415,7 +417,7 @@
 
 
 def far_kernel(msg_ref, near_ref, *refs):
-    inputs, out_ref, scratch, o_scr = refs[:15], refs[15], refs[16:-1], refs[-1]
+    inputs, out_ref, scratch, o_scr = refs[:14], refs[14], refs[15:-1], refs[-1]
     side = is_odd("gx")
     o_scr[1 - side] = near_ref[...]
 
@@ -512,17 +514,17 @@
         2 * 10**10, 10**7,
         cot, marks, pe, de, w1, w3, w4, wd, wu,
     )
-    shared = (cot, marks, pe, dve, de, gm, qm, q, parity, w1, w2, w3, w4, wd, wu)
+    shared = (cot, marks, pe, dve, de, gm, qm, q, w1, w2, w3, w4, wd, wu)
     near = call(
         near_kernel,
-        [VMEM] * 16,
+        [VMEM] * 15,
         shape(2, 256, 128, dtype=F32),
         SIDE_SCRATCH,
         2 * 10**10, 10**7, x_b, *shared,
     )
     return call(
         far_kernel,
-        [VMEM] * 17,
+        [VMEM] * 16,
         shape(32, 16, 256),
         SIDE_SCRATCH + [pltpu.VMEM((2, 2, 256, 128), F32)],
         10**10, 10**7, x_a, near, *shared,

time: 35.2 us -> 35.2 us (level)
  no operation moved by 1% of the time
where the time goes in v6:
time: 35.2 us; the launch traced here: 35 us
  starting transfers between devices  19.6 us (56%)
  Pallas kernels  13.5 us (38%)
  local copies, waits for them, and re-layouts  1.01 us (3%)
  between operations  0.85 us (2%)
    pallas_call x7, Pallas kernels, call(): pl.pallas_call(kernel, out_shape=outs, in_specs=specs, out_specs=jax.tree...  13.5 us
    ppermute x2, starting transfers between devices, swaps(): lax.ppermute(second, axis, both_ways(0))  12.4 us
    ppermute x2, starting transfers between devices, swaps(): lax.ppermute(first, axis, both_ways(1))  7.21 us
  transfers between devices with their start and end apart: 4, of which 0 were waited for; matrix products, arithmetic and copies ran while one was open for 2% of the time, Pallas kernels for 22%

profile of v6, /device:TPU:55, one launch (start us, length us, event | category | flops | bytes accessed | tf_op | source)
XLA Modules:
  0.0 35.0 jit_solution(2037280892965395752)
XLA Ops:
  0.0 0.0 copy-start.1
  0.0 0.0 copy-start
  0.0 0.1 shard_map.64
  0.8 0.1 copy-done.1
  0.9 0.1 copy-done
  1.0 0.0 copy-start.4
  1.0 0.0 copy-start.3
  1.0 0.0 copy-start.2
  1.0 0.6 %shard_map.65 = (bf16[8,64,256]{2,1,0:T(8,128)(2,1)S(1)}, bf16[4,64,128]{2,1,0:T(8,128)(2,1)S(1)}, bf16[272,256]{1,0:T(8,128)(2,1)S(1)}, bf16[272,256]{1,0:T(8,128)(2,1)S(1)}) custom-call(s32[1]{0:T(128)} %bitcast.1.flag_ref, bf16[32,16,256]{2,1,0:T(8,128)(2,1)S(1)} %copy-done, bf16[64,8,64]{2,1,0:T(8,128)(2,1)S(1)} %copy-done.1, ...), custom_call_target="tpu_custom_call" | custom-call | flops 2000000000 | bytes 1000000 | tf_op jit(solution)/shard_map/pallas_call | solution.py:447
  1.6 3.0 %collective-permute-start = (bf16[272,256]{1,0:T(8,128)(2,1)S(1)}, bf16[272,256]{1,0:T(8,128)(2,1)S(1)}, u32[]{:S(2)}, u32[]{:S(2)}) collective-permute-start(bf16[272,256]{1,0:T(8,128)(2,1)S(1)} %get-tuple-element.30), channel_id=1, source_target_pairs={{1,2},{3,4},{5,6},{7,8},{9,10},{11,12},{13,14},{2,1},{4,3},{6,5},{... | collective-permute-start | bytes 417800 | tf_op jit(solution)/shard_map/ppermute | solution.py:469
  4.6 9.2 %collective-permute-start.1 = (bf16[272,256]{1,0:T(8,128)(2,1)S(1)}, bf16[272,256]{1,0:T(8,128)(2,1)S(1)}, u32[]{:S(2)}, u32[]{:S(2)}) collective-permute-start(bf16[272,256]{1,0:T(8,128)(2,1)S(1)} %get-tuple-element.31), channel_id=1, source_target_pairs={{0,1},{2,3},{4,5},{6,7},{8,9},{10,11},{12,13},{14,15},{1,0},{3,2},... | collective-permute-start | bytes 417800 | tf_op jit(solution)/shard_map/ppermute | solution.py:469
  13.8 0.0 copy-done.4
  13.8 0.1 reshape.15.ud_ref
  13.9 0.0 copy-done.3
  13.9 0.2 reshape.13.u1_ref
  14.1 0.0 copy-done.2
  14.1 0.4 %reshape.14.u2_ref = bf16[1728,64]{1,0:T(8,128)(2,1)S(1)} reshape(bf16[27,4096]{1,0:T(8,128)(2,1)S(1)} %copy-done.2) | data formatting | bytes 442368 | tf_op jit(solution)/shard_map/reshape | solution.py:495
  14.6 3.0 %shard_map.66 = (bf16[2048,256]{1,0:T(8,128)(2,1)S(1)}, bf16[2048,256]{1,0:T(8,128)(2,1)S(1)}, bf16[2304,128]{1,0:T(8,128)(2,1)S(1)}, bf16[2304,128]{1,0:T(8,128...) custom-call(bf16[864,32]{1,0:T(8,128)(2,1)S(1)} %reshape.13.u1_ref, ...), custom_call_target="tpu_custom_call" | custom-call | flops 1000000000 | bytes 10000000 | tf_op jit(solution)/shard_map/pallas_call | solution.py:447
  17.6 0.0 collective-permute-done.ya_ref
  17.6 0.0 collective-permute-done.1.yb_ref
  17.6 1.6 %shard_map.67 = (bf16[304,256]{1,0:T(8,128)(2,1)S(1)}, bf16[304,256]{1,0:T(8,128)(2,1)S(1)}, bf16[4,96,128]{2,1,0:T(8,128)(2,1)S(1)}, bf16[128,128]{1,0:T(8,128)...) custom-call(s32[1]{0:T(128)} %bitcast.2.flag_ref, ...), custom_call_target="tpu_custom_call" | custom-call | flops 500000000 | bytes 1000000 | tf_op jit(solution)/shard_map/pallas_call | solution.py:447
  19.2 4.2 %collective-permute-start.2 = (bf16[304,256]{1,0:T(8,128)(2,1)S(1)}, bf16[304,256]{1,0:T(8,128)(2,1)S(1)}, u32[]{:S(2)}, u32[]{:S(2)}) collective-permute-start(bf16[304,256]{1,0:T(8,128)(2,1)S(1)} %get-tuple-element.34), channel_id=1, source_target_pairs={{16,32},{48,64},{80,96},{112,128},{144,160},{176,192},{208,224},{2... | collective-permute-start | bytes 466952 | tf_op jit(solution)/shard_map/ppermute | solution.py:469
  23.5 3.3 %collective-permute-start.3 = (bf16[304,256]{1,0:T(8,128)(2,1)S(1)}, bf16[304,256]{1,0:T(8,128)(2,1)S(1)}, u32[]{:S(2)}, u32[]{:S(2)}) collective-permute-start(bf16[304,256]{1,0:T(8,128)(2,1)S(1)} %get-tuple-element.35), channel_id=1, source_target_pairs={{0,16},{32,48},{64,80},{96,112},{128,144},{160,176},{192,208},{224... | collective-permute-start | bytes 466952 | tf_op jit(solution)/shard_map/ppermute | solution.py:469
  26.7 1.7 %shard_map.68 = (bf16[9,2,80,128]{3,2,1,0:T(8,128)(2,1)S(1)}, bf16[4,2,64,256]{3,2,1,0:T(8,128)(2,1)S(1)}) custom-call(bf16[4,96,128]{2,1,0:T(8,128)(2,1)S(1)} %get-tuple-element.36.cot_ref.refs_0_, bf16[128,128]{1,0:T(8,128)(2,1)S(1)} %get-tuple-element.37.marks_ref.refs_1_, bf16[4,8,112,256]{3,2,1,0:T(8,128)(2,1)S(1)} %get-tuple-element.38.p_ref.refs_2_, ...), custom_call_target="tpu_custom_call" | custom-call | flops 20000000000 | bytes 10000000 | tf_op jit(solution)/shard_map/pallas_call | solution.py:447
  28.5 0.0 collective-permute-done.3.msg_ref
  28.5 2.9 %shard_map.69.near_ref = f32[2,256,128]{2,1,0:T(8,128)S(1)} custom-call(bf16[304,256]{1,0:T(8,128)(2,1)S(1)} %collective-permute-done.3.msg_ref, bf16[4,96,128]{2,1,0:T(8,128)(2,1)S(1)} %get-tuple-element.36.cot_ref.refs_0_, bf16[128,128]{1,0:T(8,128)(2,1)S(1)} %get-tuple-element.37.marks_ref.refs_1_, ...), custom_call_target="tpu_custom_call" | custom-call | flops 20000000000 | bytes 10000000 | tf_op jit(solution)/shard_map/pallas_call | solution.py:447
  31.4 0.0 collective-permute-done.2.msg_ref
  31.4 3.6 %shard_map.70 = bf16[32,16,256]{2,1,0:T(8,128)(2,1)} custom-call(bf16[304,256]{1,0:T(8,128)(2,1)S(1)} %collective-permute-done.2.msg_ref, f32[2,256,128]{2,1,0:T(8,128)S(1)} %shard_map.69.near_ref, bf16[4,96,128]{2,1,0:T(8,128)(2,1)S(1)} %get-tuple-element.36.cot_ref.refs_0_, bf16[128,128]{1,0:T(8,128)(2,1)S(1)} %get-tuple-element.37.marks_ref.refs_1_, ...), custom_call_target="tpu_custom_call" | custom-call | flops 10000000000 | bytes 10000000 | tf_op jit(solution)/shard_map/pallas_call | solution.py:447
Async XLA Ops:
  0.0 0.9 %copy-start.1 = (bf16[64,8,64]{2,1,0:T(8,128)(2,1)S(1)}, bf16[64,8,64]{2,1,0:T(8,128)(2,1)}, u32[]{:S(2)}) copy-start(bf16[64,8,64]{2,1,0:T(8,128)(2,1)} %cot_ref.1) | copy-start | bytes 196612
  0.0 1.0 %copy-start = (bf16[32,16,256]{2,1,0:T(8,128)(2,1)S(1)}, bf16[32,16,256]{2,1,0:T(8,128)(2,1)}, u32[]{:S(2)}) copy-start(bf16[32,16,256]{2,1,0:T(8,128)(2,1)} %feat_ref.1) | copy-start | bytes 786436
  1.0 12.7 %copy-start.4 = (bf16[8,2048]{1,0:T(8,128)(2,1)S(1)}, bf16[8,2048]{1,0:T(8,128)(2,1)}, u32[]{:S(2)}) copy-start(bf16[8,2048]{1,0:T(8,128)(2,1)} %param.9) | copy-start | bytes 98308
  1.0 12.9 %copy-start.3 = (bf16[27,1024]{1,0:T(8,128)(2,1)S(1)}, bf16[27,1024]{1,0:T(8,128)(2,1)}, u32[]{:S(2)}) copy-start(bf16[27,1024]{1,0:T(8,128)(2,1)} %param.8) | copy-start | bytes 165892
  1.0 13.1 %copy-start.2 = (bf16[27,4096]{1,0:T(8,128)(2,1)S(1)}, bf16[27,4096]{1,0:T(8,128)(2,1)}, u32[]{:S(2)}) copy-start(bf16[27,4096]{1,0:T(8,128)(2,1)} %param.10) | copy-start | bytes 663556
  1.6 16.0 %collective-permute-start = (bf16[272,256]{1,0:T(8,128)(2,1)S(1)}, bf16[272,256]{1,0:T(8,128)(2,1)S(1)}, u32[]{:S(2)}, u32[]{:S(2)}) collective-permute-start(bf16[272,256]{1,0:T(8,128)(2,1)S(1)} %get-tuple-element.30), channel_id=1, source_target_pairs={{1,2},{3,4},{5,6},{7,8},{9,10},{11,12},{13,14},{2,1},{4,3},{6,5},{... | collective-permute-start | bytes 417800 | tf_op jit(solution)/shard_map/ppermute | solution.py:469
  4.6 13.0 %collective-permute-start.1 = (bf16[272,256]{1,0:T(8,128)(2,1)S(1)}, bf16[272,256]{1,0:T(8,128)(2,1)S(1)}, u32[]{:S(2)}, u32[]{:S(2)}) collective-permute-start(bf16[272,256]{1,0:T(8,128)(2,1)S(1)} %get-tuple-element.31), channel_id=1, source_target_pairs={{0,1},{2,3},{4,5},{6,7},{8,9},{10,11},{12,13},{14,15},{1,0},{3,2},... | collective-permute-start | bytes 417800 | tf_op jit(solution)/shard_map/ppermute | solution.py:469
  19.2 12.2 %collective-permute-start.2 = (bf16[304,256]{1,0:T(8,128)(2,1)S(1)}, bf16[304,256]{1,0:T(8,128)(2,1)S(1)}, u32[]{:S(2)}, u32[]{:S(2)}) collective-permute-start(bf16[304,256]{1,0:T(8,128)(2,1)S(1)} %get-tuple-element.34), channel_id=1, source_target_pairs={{16,32},{48,64},{80,96},{112,128},{144,160},{176,192},{208,224},{2... | collective-permute-start | bytes 466952 | tf_op jit(solution)/shard_map/ppermute | solution.py:469
  23.5 5.0 %collective-permute-start.3 = (bf16[304,256]{1,0:T(8,128)(2,1)S(1)}, bf16[304,256]{1,0:T(8,128)(2,1)S(1)}, u32[]{:S(2)}, u32[]{:S(2)}) collective-permute-start(bf16[304,256]{1,0:T(8,128)(2,1)S(1)} %get-tuple-element.35), channel_id=1, source_target_pairs={{0,16},{32,48},{64,80},{96,112},{128,144},{160,176},{192,208},{224... | collective-permute-start | bytes 466952 | tf_op jit(solution)/shard_map/ppermute | solution.py:469
